TPU v7x, 256 devices: a whole 4x4x8 slice. The times are simulated.
256 devices in a mesh: group: 8 (over z_hi, x), shard: 32 (over y, z_lo, core).
Axes of the slice: x: 4, y: 4, z: 8 (z_hi: 2, z_lo: 4; z = z_hi * 4 + z_lo), core: 2. Of those that a mesh axis runs over, the one named last changes fastest.
Arguments:
- top_input: bfloat16 [32768, 3456], P(('group', 'shard')), may hold values from -6 to 6
- pre_act: bfloat16 [32768, 512], P(('group', 'shard')), may hold values from -6 to 6
- grad_hidden: bfloat16 [32768, 512], P(('group', 'shard')), may hold values from -6 to 6
- top_weight: bfloat16 [3456, 512], replicated, may hold values from -0.109375 to 0.109375
- core_first: bfloat16 [1024, 256], replicated, may hold values from -1 to 1
- core_mid: bfloat16 [1024, 2048], replicated, may hold values from -1 to 1
- core_last: bfloat16 [1024, 256], replicated, may hold values from -1 to 1
- bag_ids: int32 [8, 32, 4096], P('group', 'shard'), may hold values from 0 to 3327, never falling along the last dimension, each value on 1 to 8 neighbouring positions
- lookup_order: int32 [8, 32, 4096], P('group', 'shard'), may hold values from 0 to 4095, each once within a row
- hot_rows: int32 [8, 32, 3072], P('group', 'shard'), may hold values from 0 to 2047
- cold_digits: int32 [8, 32, 3, 1024], P('group', 'shard'), may hold values from 0 to 1023, as said below
Outputs:
- hot_grad: float32 [8, 65536, 128], P('group', 'shard')
- dense_grad: bfloat16 [32768, 128], P(('group', 'shard'))
- weight_grad: float32 [3456, 512], P('shard', 'group')
- first_grad: float32 [1024, 256], P('shard', 'group')
- mid_grad: float32 [1024, 2048], P('shard', 'group')
- last_grad: float32 [1024, 256], P('shard', 'group')
Inputs may be any that keep to these rules, and one draw needn't show every extreme that they name: `bag_ids`: each device's lookups come in bag order; every one of its 3328 bags has 1 to 8 lookups. `lookup_order`: a permutation of each device's lookups: the first 3072 are hot, exactly 96 to each owner along shard in owner order, the rest cold. `cold_digits`: the j-th cold lookup of a device has its second digit in the block of 32 values numbered j // 32; first and third digits unconstrained.
All inputs are finite; a program needn't handle non-finite values.
Results may differ from a plain program's by a relative error of at most 0.0049.
Values may be sent and summed in bfloat16 or wider, within the bound.
A program may use at most 128 MiB of HBM per device.

v0:
```python
import jax
import jax.numpy as jnp
from jax import lax
from jax.sharding import PartitionSpec as P

E = 128
RANK = 32
NDIG = 1024
E1 = 8
E2 = 2
ROWS_DEV = 2048
E3 = 8
COLD_N = 1024
HOT_N = 3072


def by_digit(digits, terms_cols, count):
    table = lax.broadcasted_iota(jnp.int32, (count, digits.shape[0]), 0)
    onehot = (table == digits[None, :]).astype(jnp.bfloat16)
    return lax.dot_general(
        onehot, terms_cols, (((1,), (1,)), ((), ())), preferred_element_type=jnp.float32
    )


def gather_cols(core_cols, digits):
    return jnp.take(core_cols, digits, axis=1)


def grad_cols(flat_rows):
    count = flat_rows.shape[0]
    return flat_rows.T.astype(jnp.float32).reshape(E1, E2, E3, count)


def middle_terms(grad_wide, first_cols, last_cols):
    count = grad_wide.shape[-1]
    first_wide = first_cols.astype(jnp.float32).reshape(E1, RANK, count)
    last_wide = last_cols.astype(jnp.float32).reshape(RANK, E3, count)
    prod_h = jnp.sum(first_wide[:, :, None, None, :] * grad_wide[:, None, :, :, :], axis=0)
    term_mid = jnp.sum(prod_h[:, :, None, :, :] * last_wide[None, None, :, :, :], axis=3)
    return term_mid.astype(jnp.bfloat16).reshape(RANK * E2 * RANK, count)


def body(
    top_input,
    pre_act,
    grad_hidden,
    top_weight,
    core_first,
    core_mid,
    core_last,
    bag_ids,
    lookup_order,
    hot_rows,
    cold_digits,
):
    shards = lax.axis_size("shard")
    per_owner = HOT_N // shards
    pre_grad = jnp.where(pre_act > 0, grad_hidden, jnp.zeros_like(grad_hidden))
    input_grad = jnp.einsum("bh,dh->bd", pre_grad, top_weight, preferred_element_type=jnp.float32)
    dense_grad = input_grad[:, :E].astype(jnp.bfloat16)
    pooled = input_grad[:, E:].astype(jnp.bfloat16).reshape(-1, E)
    bags = bag_ids[0, 0]
    order = lookup_order[0, 0]
    sent = pooled[bags[order[:HOT_N]]].reshape(shards, per_owner, E)
    targets = hot_rows[0, 0].reshape(shards, per_owner)
    arrived, arrived_rows = (
        lax.all_to_all(sent, "shard", split_axis=0, concat_axis=0, tiled=True),
        lax.all_to_all(targets, "shard", split_axis=0, concat_axis=0, tiled=True),
    )
    hot_grad = jax.ops.segment_sum(
        arrived.reshape(-1, E).astype(jnp.float32), arrived_rows.reshape(-1), num_segments=ROWS_DEV
    )
    weight_local = jnp.einsum("bd,bh->dh", top_input, pre_grad, preferred_element_type=jnp.float32)
    digits = cold_digits[0, 0]
    cold_flat = pooled[bags[order[HOT_N:]]]
    first_table = core_first.T
    mid_table = core_mid.T
    last_table = core_last.T
    grad_wide = grad_cols(cold_flat)
    first_cols = gather_cols(first_table, digits[0])
    last_cols = gather_cols(last_table, digits[2])
    first_wide = first_cols.astype(jnp.float32).reshape(E1, RANK, COLD_N)
    last_wide = last_cols.astype(jnp.float32).reshape(RANK, E3, COLD_N)
    mid_wide = gather_cols(mid_table, digits[1]).astype(jnp.float32).reshape(RANK, E2, RANK, COLD_N)
    prod_p = jnp.sum(first_wide[:, :, None, None, :] * mid_wide[None, :, :, :, :], axis=1)
    prod_q = jnp.sum(mid_wide[:, :, :, None, :] * last_wide[None, None, :, :, :], axis=2)
    term_first = jnp.sum(grad_wide[:, None, :, :, :] * prod_q[None, :, :, :, :], axis=(2, 3))
    term_last = jnp.sum(prod_p[:, :, :, None, :] * grad_wide[:, :, None, :, :], axis=(0, 1))
    term_first = term_first.astype(jnp.bfloat16).reshape(E1 * RANK, COLD_N)
    term_last = term_last.astype(jnp.bfloat16).reshape(RANK * E3, COLD_N)
    first_local = by_digit(digits[0], term_first, NDIG)
    last_local = by_digit(digits[2], term_last, NDIG)
    term_mid = middle_terms(grad_wide, first_cols, last_cols)
    mid_local = by_digit(digits[1], term_mid, NDIG)
    local_sums = (weight_local, first_local, last_local, mid_local)
    row_parts = (
        lax.psum_scatter(local_sums[0], "shard", scatter_dimension=0, tiled=True),
        lax.psum_scatter(local_sums[1], "shard", scatter_dimension=0, tiled=True),
        lax.psum_scatter(local_sums[2], "shard", scatter_dimension=0, tiled=True),
        lax.psum_scatter(local_sums[3], "shard", scatter_dimension=0, tiled=True),
    )
    totals = (
        lax.psum_scatter(row_parts[0], "group", scatter_dimension=1, tiled=True),
        lax.psum_scatter(row_parts[1], "group", scatter_dimension=1, tiled=True),
        lax.psum_scatter(row_parts[2], "group", scatter_dimension=1, tiled=True),
        lax.psum_scatter(row_parts[3], "group", scatter_dimension=1, tiled=True),
    )
    weight_grad = totals[0]
    first_grad = totals[1]
    last_grad = totals[2]
    mid_grad = totals[3]
    return (hot_grad[None], dense_grad, weight_grad, first_grad, mid_grad, last_grad)


def solution(mesh):
    return jax.shard_map(
        body,
        mesh=mesh,
        in_specs=(
            P(("group", "shard"), None),
            P(("group", "shard"), None),
            P(("group", "shard"), None),
            P(),
            P(),
            P(),
            P(),
            P("group", "shard", None),
            P("group", "shard", None),
            P("group", "shard", None),
            P("group", "shard", None, None),
        ),
        out_specs=(
            P("group", "shard", None),
            P(("group", "shard"), None),
            P("shard", "group"),
            P("shard", "group"),
            P("shard", "group"),
            P("shard", "group"),
        ),
        check_vma=False,
    )
```

profile of v0, /device:TPU:6, one launch (start us, length us, event | category | flops | bytes accessed | tf_op | source)
XLA Modules:
  0.0 1217.4 jit_solution(12259108905153394954)
XLA Ops:
  13.0 5.8 gather_fusion.2
  20.8 6.0 gather_fusion.6
  31.5 6.0 gather_fusion.5
  50.9 11.6 gather_fusion.4
  62.5 6.5 copy.33
  71.6 6.0 select_convert_fusion
  77.6 32.3 %multiply_reduce_fusion.1 = (bf16[32,2,32,1024]{3,2,1,0:T(8,128)(2,1)}, f32[32,2,8,1024]{3,2,1,0:T(8,128)}) fusion(f32[32,2,8,1024]{3,2,1,0:T(8,128)S(1)} %multiply_reduce_fusion.4, f32[32,8,1024]{2,1,0:T(8,128)} %bitcast.66, f32[32,2,32,1024]{3,2,1,0:T(8,128)} %select_convert_fusion), kind=kLoop, calls=%fused_computation.9 | loop fusion | flops 64487424 | bytes 17825792 | tf_op jit(solution)/shard_map/reduce_sum | solution.py:39
  109.9 6.3 multiply_reduce_fusion.5
  118.2 7.5 multiply_reduce_fusion
  129.0 4.0 convolution_bitcast_fusion
  133.6 8.9 fusion.1
  144.6 8.9 all-to-all-start
  153.6 17.4 %gather_fusion = s32[3072]{0:T(1024)S(1)} fusion(s32[4096]{0:T(1024)S(1)} %bitcast.54, s32[3072]{0:T(1024)S(1)} %broadcast_clamp_fusion.1), kind=kCustom, calls=%fused_computation.2 | custom fusion | bytes 36864 | tf_op jit(solution)/shard_map/gather | solution.py:64
  171.7 13.4 %gather_fusion.1 = bf16[3072,128]{1,0:T(8,128)(2,1)} fusion(bf16[3328,128]{1,0:T(8,128)(2,1)} %copy-done.3, s32[3072]{0:T(1024)} %broadcast_clamp_fusion), kind=kCustom, calls=%fused_computation.3 | custom fusion | bytes 1585152 | tf_op jit(solution)/shard_map/gather | solution.py:64
  185.0 7.8 all-to-all-start.1
  192.9 74.4 %reduce-scatter.15.cloned.1.call-done = f32[32,256]{1,0:T(8,128)} async-done(((f32[1024,256]{1,0:T(8,128)}), f32[32,256]{1,0:T(8,128)}) %reduce-scatter.15.cloned.1.call-update) | async-done | bytes 32784 | tf_op jit(solution)/shard_map/reduce_scatter | solution.py:98
  270.8 141.0 %reduce-scatter.21.cloned.1.call-done = f32[32,256]{1,0:T(8,128)} async-done(((f32[1024,256]{1,0:T(8,128)}), f32[32,256]{1,0:T(8,128)}) %reduce-scatter.21.cloned.1.call-update) | async-done | bytes 32784 | tf_op jit(solution)/shard_map/reduce_scatter | solution.py:99
  413.4 303.4 %all-reduce.3.cloned.1.call-done = f32[3456,512]{0,1:T(8,128)} async-done(((f32[3456,512]{0,1:T(8,128)}), f32[3456,512]{0,1:T(8,128)}) %all-reduce.3.cloned.1.call-update) | async-done | bytes 7077904
  718.8 159.9 %reduce-scatter.17.cloned.1.call-done = f32[32,2048]{1,0:T(8,128)} async-done(((f32[1024,2048]{1,0:T(8,128)}), f32[32,2048]{1,0:T(8,128)}) %reduce-scatter.17.cloned.1.call-update) | async-done | bytes 262160 | tf_op jit(solution)/shard_map/reduce_scatter | solution.py:100
  882.1 18.3 %scatter_custom_fusion = f32[2048,128]{1,0:T(8,128)} fusion(s32[3072]{0:T(1024)} %reshape.257, bf16[3072,128]{1,0:T(8,128)(2,1)} %bitcast.38, f32[]{:T(128)} %constant.7.clone.1), kind=kCustom, calls=%fused_computation.26 | custom fusion | flops 786432 | bytes 1835520 | tf_op jit(solution)/shard_map/scatter-add | solution.py:70
  900.4 59.8 %reduce-scatter.23.cloned.1.call-done = f32[32,32]{1,0:T(8,128)} async-done(((f32[256,32]{1,0:T(8,128)}), f32[32,32]{1,0:T(8,128)}) %reduce-scatter.23.cloned.1.call-update) | async-done | bytes 4112
  961.7 81.1 %reduce-scatter.25.cloned.1.call-done = f32[32,32]{1,0:T(8,128)} async-done(((f32[256,32]{1,0:T(8,128)}), f32[32,32]{1,0:T(8,128)}) %reduce-scatter.25.cloned.1.call-update) | async-done | bytes 4112
  1044.2 82.2 %reduce-scatter.13.cloned.1.call-done = f32[108,64]{0,1:T(8,128)} async-done(((f32[108,512]{0,1:T(8,128)}), f32[108,64]{0,1:T(8,128)}) %reduce-scatter.13.cloned.1.call-update) | async-done | bytes 27664 | tf_op jit(solution)/shard_map/reduce_scatter | solution.py:103
  1126.4 84.1 %reduce-scatter.19.cloned.1.call-done = f32[32,256]{1,0:T(8,128)} async-done(((f32[32,2048]{1,0:T(8,128)}), f32[32,256]{1,0:T(8,128)}) %reduce-scatter.19.cloned.1.call-update) | async-done | bytes 32784 | tf_op jit(solution)/shard_map/reduce_scatter | solution.py:106
  (90 shorter events, 49.7 us)
Async XLA Ops:
  7.2 35.2 %copy-start = (bf16[3456,512]{1,0:T(8,128)(2,1)S(1)}, bf16[3456,512]{1,0:T(8,128)(2,1)}, u32[]{:S(2)}) copy-start(bf16[3456,512]{1,0:T(8,128)(2,1)} %param.16) | copy-start | bytes 10616836
  7.2 260.2 %reduce-scatter.15.cloned.1.call-start = ((), (), s32[]{:S(2)}) async-start(), calls=%async_computation.10 | async-start | bytes 1081344 | tf_op jit(solution)/shard_map/reduce_scatter | solution.py:98
  44.6 0.9 copy-start.6
  46.7 15.8 %copy-start.3 = (bf16[3328,128]{1,0:T(8,128)(2,1)}, bf16[3328,128]{1,0:T(8,128)(2,1)S(1)}, u32[]{:S(2)}) copy-start(bf16[3328,128]{1,0:T(8,128)(2,1)S(1)} %reshape.193) | copy-start | bytes 2555908
  62.5 6.5 copy-start.4
  62.5 9.1 copy-start.14
  118.1 7.6 copy-start.5
  118.1 293.7 %reduce-scatter.21.cloned.1.call-start = ((), (), s32[]{:S(2)}) async-start(), calls=%async_computation.13 | async-start | bytes 1081344 | tf_op jit(solution)/shard_map/reduce_scatter | solution.py:99
  125.7 3.3 copy-start.7
  125.7 3.3 copy-start.8
  125.7 3.3 copy-start.9
  128.9 588.0 %all-reduce.3.cloned.1.call-start = ((), (), s32[]{:S(2)}) async-start(), calls=%async_computation.16 | async-start | bytes 14155776
  133.0 745.7 %reduce-scatter.17.cloned.1.call-start = ((), (), s32[]{:S(2)}) async-start(), calls=%async_computation.11 | async-start | bytes 8650752 | tf_op jit(solution)/shard_map/reduce_scatter | solution.py:100
  142.5 0.7 copy-start.13
  142.5 11.0 copy-start.11
  142.5 11.1 copy-start.2
  144.6 40.4 %all-to-all-start = ((s32[32,1,96]{2,1,0:T(1,128)}), s32[32,1,96]{2,1,0:T(1,128)S(1)}, u32[]{:S(2)}, u32[]{:S(2)}) async-start(s32[32,1,96]{2,1,0:T(1,128)} %all_to_all.9), calls=%async_computation | async-start | bytes 32768 | tf_op jit(solution)/shard_map/all_to_all | solution.py:68
  171.7 1038.8 %copy-start.1 = (bf16[3456,512]{1,0:T(8,128)(2,1)S(1)}, bf16[3456,512]{1,0:T(8,128)(2,1)}, u32[]{:S(2)}) copy-start(bf16[3456,512]{1,0:T(8,128)(2,1)} %param.16) | copy-start | bytes 10616836
  185.0 693.6 %copy-start.10 = (s32[32,1,96]{2,1,0:T(1,128)}, s32[32,1,96]{2,1,0:T(1,128)S(1)}, u32[]{:S(2)}) copy-start(s32[32,1,96]{2,1,0:T(1,128)S(1)} %all-to-all-done) | copy-start | bytes 36868
  185.0 697.1 %all-to-all-start.1 = ((bf16[32,96,128]{2,1,0:T(8,128)(2,1)}), bf16[32,96,128]{2,1,0:T(8,128)(2,1)}, u32[]{:S(2)}, u32[]{:S(2)}) async-start(bf16[32,96,128]{2,1,0:T(8,128)(2,1)} %bitcast.67), calls=%async_computation.1 | async-start | bytes 1572864 | tf_op jit(solution)/shard_map/all_to_all | solution.py:67
  192.9 767.4 %reduce-scatter.23.cloned.1.call-start = ((), (), s32[]{:S(2)}) async-start(), calls=%async_computation.14 | async-start | bytes 147456
  268.9 773.9 %reduce-scatter.25.cloned.1.call-start = ((), (), s32[]{:S(2)}) async-start(), calls=%async_computation.15 | async-start | bytes 147456
  413.3 713.1 %reduce-scatter.13.cloned.1.call-start = ((), (), s32[]{:S(2)}) async-start(), calls=%async_computation.9 | async-start | bytes 294912 | tf_op jit(solution)/shard_map/reduce_scatter | solution.py:103
  718.7 491.8 %reduce-scatter.19.cloned.1.call-start = ((), (), s32[]{:S(2)}) async-start(), calls=%async_computation.12 | async-start | bytes 294912 | tf_op jit(solution)/shard_map/reduce_scatter | solution.py:106
  (1 other events, 0.7 us)
Sparse Core Ops, SparseCore 0:
  118.2 149.0 reduce-scatter.14
  270.0 141.7 reduce-scatter.20
  414.5 302.2 all-reduce.2
  719.2 159.3 reduce-scatter.16
  882.3 77.9 reduce-scatter.22
  964.0 78.7 reduce-scatter.24
  1047.2 79.1 reduce-scatter.12
  1131.3 79.1 reduce-scatter.18
where the time goes:
time: 1220 us
  waiting for transfers between devices  986 us (81%)
  local copies, waits for them, and re-layouts  92.3 us (8%)
  other arithmetic  88 us (7%)
  matrix products  18.8 us (2%)
  starting transfers between devices  17.1 us (1%)
  between operations  15.1 us (1%)
    unnamed x11, waiting for transfers between devices  445 us
    reduce_scatter x1, waiting for transfers between devices, body(): lax.psum_scatter(local_sums[3], 'shard', scatter_dimension=0, tiled=True)  160 us
    reduce_scatter x1, waiting for transfers between devices, body(): lax.psum_scatter(local_sums[2], 'shard', scatter_dimension=0, tiled=True)  141 us
    reduce_scatter x1, waiting for transfers between devices, body(): lax.psum_scatter(row_parts[3], 'group', scatter_dimension=1, tiled=True)  84.1 us
    reduce_scatter x1, waiting for transfers between devices, body(): lax.psum_scatter(row_parts[0], 'group', scatter_dimension=1, tiled=True)  82.2 us
    reduce_scatter x1, waiting for transfers between devices, body(): lax.psum_scatter(local_sums[1], 'shard', scatter_dimension=0, tiled=True)  74.4 us
    reduce_sum x1, other arithmetic, middle_terms(): jnp.sum(prod_h[:, :, None, :, :] * last_wide[None, None, :, :, :], axis=3)  32.3 us
    gather x2, local copies, waits for them, and re-layouts, body(): sent = pooled[bags[order[:HOT_N]]].reshape(shards, per_owner, E)  30.8 us
  transfers between devices with their start and end apart: 10, of which 8 were waited for; matrix products, arithmetic and copies ran while one was open for 7% of the time, Pallas kernels for 0%

commit v1 on v0

v1 whole, which is shorter than its diff:
```python
import functools

import jax
import jax.numpy as jnp
from jax import lax
from jax.experimental import pallas as pl
from jax.experimental.pallas import tpu as pltpu
from jax.sharding import PartitionSpec as P

F32 = jnp.float32
BF16 = jnp.bfloat16
I32 = jnp.int32

E = 128
RANK = 32
E1 = 8
E2 = 2
E3 = 8
HOT_N = 3072
SHARDS = 32
GROUPS = 8
PER_HOT = 96
PER_COLD = 32
BLOCK_W = 108
PAD_W = 112
ROWS = PAD_W + 32
MESH = pl.DeviceIdType.MESH


def iota(shape, dim):
    return lax.broadcasted_iota(I32, shape, dim)


def dot(a, b):
    return jnp.dot(a, b, preferred_element_type=F32)


def dot_nt(a, b):
    return lax.dot_general(a, b, (((1,), (1,)), ((), ())), preferred_element_type=F32)


def zero_one(mask):
    return jnp.where(mask, 1.0, 0.0).astype(BF16)


def kernel(
    act_ref, hid_ref, tw_ref, x_ref, rowmap, order, meta_ref, first_ref, last_ref, midq_ref, midl_ref,
    dense_ref, hot_ref, wout_ref, fout_ref, lout_ref, mout_ref,
    pooled, stage, send_c, send_h, recv_c, recv_h, recv_m,
    xt, xt_recv, pre2, w_own, ring,
    first_t, last_t, onehot, a_t, c_t, q_t, he, ce, qs, tnat, terms, mid_acc, mid_send, mid_recv,
    fl_own, fl_send, fl_recv, fx, fx_recv,
    ybuf, y_recv, zbuf, z_recv, h_send, h_recv,
    core_s, core_r, a_s, a_r, ring_s, ring_r, f_s, f_r, y_s, y_r, z_s, z_r, h_s, h_r, m_s, m_r,
):
    g = lax.axis_index("group")
    s = lax.axis_index("shard")
    xx = lax.rem(g, 4)
    zh = g // 4
    core = lax.rem(s, 2)
    zl = lax.rem(s // 2, 4)
    yy = s // 8

    def shard_at(y, z, c):
        return y * 8 + z * 2 + c

    def remote(src, dst, send_sem, recv_sem, to):
        return pltpu.make_async_remote_copy(
            src_ref=src, dst_ref=dst, send_sem=send_sem, recv_sem=recv_sem, device_id=to, device_id_type=MESH
        )

    partner = (g, shard_at(yy, zl, 1 - core))

    barrier = pltpu.get_barrier_semaphore()

    def greet_shard(k, carry):
        pl.semaphore_signal(barrier, inc=1, device_id=(g, lax.rem(s + k, SHARDS)), device_id_type=MESH)
        return carry

    def greet_group(k, carry):
        pl.semaphore_signal(barrier, inc=1, device_id=(lax.rem(g + k, GROUPS), s), device_id_type=MESH)
        return carry

    lax.fori_loop(1, SHARDS, greet_shard, 0)
    lax.fori_loop(1, GROUPS, greet_group, 0)

    pre = jnp.where(act_ref[...].astype(F32) > 0, hid_ref[...].astype(F32), 0.0).astype(BF16)
    col = iota((512, 512), 1)
    source = (col // 64 % 2) * 256 + (col // 128) * 64 + col % 64
    pre2[0:128, :] = dot(pre, zero_one(iota((512, 512), 0) == source)).astype(BF16)

    for shard in range(SHARDS):
        lo = shard * BLOCK_W // 128 * 128
        off = shard * BLOCK_W - lo
        width = 128 if off + BLOCK_W <= 128 else 256
        pick = zero_one(iota((PAD_W, width), 1) == iota((PAD_W, width), 0) + off)
        xt[shard % 2, shard // 2] = dot_nt(pick, x_ref[:, lo : lo + width]).astype(BF16)

    pl.semaphore_wait(barrier, SHARDS - 1 + GROUPS - 1)

    send_pre = remote(pre2.at[0:128], pre2.at[128:256], core_s.at[0], core_r.at[0], partner)
    send_pre.start()
    send_xt = remote(xt.at[1 - core], xt_recv, core_s.at[1], core_r.at[1], partner)
    send_xt.start()

    dense_ref[...] = dot_nt(pre, tw_ref[0:128, :]).astype(BF16)

    def pool(i, carry):
        rows = tw_ref[pl.ds(pl.multiple_of(128 + i * 256, 128), 256), :]
        part = dot_nt(pre, rows).astype(BF16).astype(F32)
        pooled[pl.ds(pl.multiple_of(i * 256, 128), 128), :] = part[:, 0:128]
        pooled[pl.ds(pl.multiple_of(i * 256 + 128, 128), 128), :] = part[:, 128:256]
        return carry

    lax.fori_loop(0, 13, pool, 0)

    send_pre.wait()
    send_xt.wait()
    pre_both = pre2[...]

    def product(j, carry):
        both = jnp.concatenate([xt[core, j], xt_recv[j]], axis=1)
        part = dot(both, pre_both).astype(BF16)
        for k in range(4):
            w_own[k, j] = part[:, k * 128 : (k + 1) * 128]
        return carry

    lax.fori_loop(0, 16, product, 0)

    right = (zh * 4 + lax.rem(xx + 1, 4), s)
    left = (zh * 4 + lax.rem(xx + 3, 4), s)

    def ring_copy(way, step):
        to = right if way == 0 else left
        if step == 0:
            chunk = lax.rem(xx + 3, 4) if way == 0 else lax.rem(xx + 1, 4)
            src = w_own.at[chunk, pl.ds(way * 8, 8)]
        else:
            src = ring.at[way, step - 1]
        return remote(src, ring.at[way, step], ring_s.at[way, step], ring_r.at[way, step], to)

    def ring_add(way, step):
        chunk = lax.rem(xx + 2 - step, 4) if way == 0 else lax.rem(xx + 2 + step, 4)

        def add(j, carry):
            total = ring[way, step, j].astype(F32) + w_own[chunk, way * 8 + j].astype(F32)
            ring[way, step, j] = total.astype(BF16)
            return carry

        lax.fori_loop(0, 8, add, 0)

    def ring_next(step):
        for way in range(2):
            ring_copy(way, step - 1).wait()
            ring_add(way, step - 1)
            ring_copy(way, step).start()

    for way in range(2):
        ring_copy(way, 0).start()

    def gather(base, count):
        for j in range(count):
            r = rowmap[order[base + j]]
            stage[pl.ds(j, 1), :] = pooled[pl.ds(r, 1), :]
        return stage[0:count, :].astype(BF16)

    def cold_to(k, carry):
        o = lax.rem(s + k, SHARDS)
        send_c[k] = gather(HOT_N + o * PER_COLD, PER_COLD)
        remote(send_c.at[k], recv_c.at[s], a_s.at[0], a_r.at[0], (g, o)).start()
        remote(meta_ref.at[o], recv_m.at[s], a_s.at[1], a_r.at[1], (g, o)).start()
        return carry

    def hot_to(k, carry):
        o = lax.rem(s + k, SHARDS)
        send_h[k] = gather(o * PER_HOT, PER_HOT)
        remote(send_h.at[k], recv_h.at[s], a_s.at[2], a_r.at[2], (g, o)).start()
        return carry

    lax.fori_loop(1, SHARDS, cold_to, 0)
    send_c[0] = gather(HOT_N + s * PER_COLD, PER_COLD)
    pltpu.make_async_copy(send_c.at[0], recv_c.at[s], a_r.at[0]).start()
    pltpu.make_async_copy(meta_ref.at[s], recv_m.at[s], a_r.at[1]).start()
    lax.fori_loop(1, SHARDS, hot_to, 0)
    send_h[0] = gather(s * PER_HOT, PER_HOT)
    pltpu.make_async_copy(send_h.at[0], recv_h.at[s], a_r.at[2]).start()

    ring_next(1)

    eye = zero_one(iota((256, 256), 0) == iota((256, 256), 1))
    first_t[...] = dot_nt(eye, first_ref[...]).astype(BF16)
    turn_row = iota((256, 256), 0)
    turn = zero_one(iota((256, 256), 1) == (turn_row % 32) * 8 + turn_row // 32)
    last_t[...] = dot_nt(turn, last_ref[...]).astype(BF16)
    mid_acc[...] = jnp.zeros_like(mid_acc)

    pltpu.make_async_copy(recv_c, recv_c, a_r.at[0]).wait()
    pltpu.make_async_copy(recv_m, recv_m, a_r.at[1]).wait()

    def cold_tile(t, carry):
        lanes = pl.ds(pl.multiple_of(t * 128, 128), 128)
        lanes_last = pl.ds(pl.multiple_of(1024 + t * 128, 128), 128)

        def digits(row):
            four = recv_m[pl.ds(4 * t, 4), row : row + 1, :]
            return four[0] + four[1] + four[2] + four[3]

        one, two, three = digits(3), digits(4), digits(5)
        for k in range(4):
            rows = slice(k * 256, (k + 1) * 256)
            place = iota((256, 128), 0) + k * 256
            onehot[rows, lanes] = zero_one(place == one)
            onehot[rows, lanes_last] = zero_one(place == three)
        a_t[...] = dot(first_t[...], onehot[:, lanes])
        c_t[...] = dot(last_t[...], onehot[:, lanes_last])
        q_t[...] = recv_c[pl.ds(4 * t, 4)].reshape(128, 128).astype(F32).T
        low, high = two % 4, two // 4
        low2 = jnp.concatenate([low, low], axis=1)
        high2 = jnp.concatenate([high, high], axis=1)
        for pair in range(4):
            cols = slice(pair * 256, (pair + 1) * 256)
            for e2 in range(2):
                halves = []
                for e3 in (2 * pair, 2 * pair + 1):
                    total = None
                    for e1 in range(8):
                        q_row = e1 * 16 + e2 * 8 + e3
                        term = a_t[e1 * 32 : (e1 + 1) * 32, :] * q_t[q_row : q_row + 1, :]
                        total = term if total is None else total + term
                    halves.append(total)
                h = jnp.concatenate(halves, axis=1)
                for k in range(4):
                    he[k * 64 + e2 * 32 : k * 64 + e2 * 32 + 32, cols] = jnp.where(low2 == k, h, 0.0).astype(BF16)
            c = jnp.concatenate(
                [c_t[e3 * 32 : (e3 + 1) * 32, :] for e3 in (2 * pair, 2 * pair + 1)], axis=1
            )
            for k in range(8):
                ce[k * 32 : (k + 1) * 32, cols] = jnp.where(high2 == k, c, 0.0).astype(BF16)
            q_all = dot(midq_ref[...], ce[:, cols])
            total = jnp.zeros((64, 256), F32)
            for k in range(4):
                total = total + jnp.where(low2 == k, q_all[k * 64 : (k + 1) * 64, :], 0.0)
            qs[:, cols] = total
            l_all = dot(midl_ref[...], he[:, cols])
            total = jnp.zeros((32, 256), F32)
            for k in range(8):
                total = total + jnp.where(high2 == k, l_all[k * 32 : (k + 1) * 32, :], 0.0)
            total = total.astype(BF16)
            tnat[256 + pair * 64 : 256 + pair * 64 + 32, lanes] = total[:, 0:128]
            tnat[256 + pair * 64 + 32 : 256 + pair * 64 + 64, lanes] = total[:, 128:256]
        mid_acc[...] += dot_nt(he[...], ce[...])
        for e1 in range(8):
            total = None
            for e2 in range(2):
                for e3 in range(8):
                    q_row = e1 * 16 + e2 * 8 + e3
                    term = qs[e2 * 32 : (e2 + 1) * 32, e3 * 128 : (e3 + 1) * 128] * q_t[q_row : q_row + 1, :]
                    total = term if total is None else total + term
            tnat[e1 * 32 : (e1 + 1) * 32, lanes] = total.astype(BF16)
        return carry

    lax.fori_loop(0, 4, cold_tile, 0)
    ring_next(2)
    lax.fori_loop(4, 8, cold_tile, 0)

    row = iota((256, 256), 0)
    source = (row // 2 % 4) * 64 + (row % 2) * 32 + ((row // 32 % 2) * 4 + row // 64) * 4 + row // 8 % 4
    moved = dot(zero_one(iota((256, 256), 1) == source), mid_acc[...].astype(BF16)).astype(BF16)
    for k in range(8):
        mid_send[k] = moved[k * 32 : (k + 1) * 32, :]

    def mid_copy(d):
        to = lax.rem(g + d, GROUPS)
        src = mid_send.at[lax.rem(to, 4) * 2 + to // 4]
        return remote(src, mid_recv.at[d - 1], m_s.at[d - 1], m_r.at[d - 1], (to, s))

    for d in range(1, GROUPS):
        mid_copy(d).start()

    row = iota((512, 256), 0)
    owner = (row // 64 % 2) * 4 + row // 128
    is_first = row % 64 < 32
    j = row % 32
    lane = iota((512, 256), 1)
    place_first = zero_one(is_first & (lane == owner * 32 + j))
    place_last = zero_one((row % 64 >= 32) & (lane == (j % 8) * 32 + owner * 4 + j // 8))
    for k in range(4):
        cols = slice(k * 256, (k + 1) * 256)
        terms[:, cols] = dot(place_first, tnat[0:256, cols]).astype(BF16)
        terms[:, 1024 + k * 256 : 1024 + (k + 1) * 256] = dot(place_last, tnat[256:512, cols]).astype(BF16)

    def by_digit(k, carry):
        part = dot_nt(onehot[pl.ds(pl.multiple_of(k * 256, 256), 256), :], terms[...])
        for i in range(4):
            for c in range(2):
                fl_own[c, 4 * k + i] = part[(2 * i + c) * 32 : (2 * i + c + 1) * 32, :]
        return carry

    lax.fori_loop(0, 4, by_digit, 0)

    def fl_round(j, carry):
        fl_send[j] = fl_own[1 - core, j].astype(BF16)
        return carry

    lax.fori_loop(0, 16, fl_round, 0)
    fl_copy = remote(fl_send, fl_recv, core_s.at[2], core_r.at[2], partner)
    fl_copy.start()

    pltpu.make_async_copy(recv_h, recv_h, a_r.at[2]).wait()
    hot_ref[...] = jnp.zeros_like(hot_ref)

    def hot_part(i, carry):
        ids = []
        for half in range(2):
            four = recv_m[pl.ds(8 * i + 4 * half, 4), :, :]
            four = four[0] + four[1] + four[2] + four[3]
            ids += [four[k : k + 1, :] for k in range(3)]
        values = recv_h[pl.ds(8 * i, 8)].reshape(768, 128).astype(F32)
        low = jnp.concatenate(ids, axis=1) % 512
        pick = zero_one(iota((512, 768), 0) == low)
        column = jnp.concatenate(
            [jnp.broadcast_to((r // 512).astype(F32), (128, 128)).T for r in ids], axis=0
        )
        for k in range(4):
            part = jnp.where(column == float(k), values, 0.0).astype(BF16)
            hot_ref[k * 512 : (k + 1) * 512, :] += dot(pick, part)
        return carry

    lax.fori_loop(0, 4, hot_part, 0)

    fl_copy.wait()

    def fl_pair(j, carry):
        total = (fl_own[core, j] + fl_recv[j].astype(F32)).astype(BF16)
        for k in range(4):
            fx[k, j] = total[:, k * 128 : (k + 1) * 128]
        return carry

    lax.fori_loop(0, 16, fl_pair, 0)

    def fl_x(d):
        to = lax.rem(xx + d, 4)
        return remote(fx.at[to], fx_recv.at[d - 1], f_s.at[d - 1], f_r.at[d - 1], (zh * 4 + to, s))

    for d in range(1, 4):
        fl_x(d).start()

    for way in range(2):
        ring_copy(way, 2).wait()

        def last_add(j, carry):
            total = ring[way, 2, j].astype(F32) + w_own[xx, way * 8 + j].astype(F32)
            ybuf[way * 8 + j, 0:PAD_W, :] = total.astype(BF16)
            return carry

        lax.fori_loop(0, 8, last_add, 0)

    for d in range(1, 4):
        fl_x(d).wait()

    def fl_x_add(j, carry):
        total = fx[xx, j].astype(F32)
        for d in range(3):
            total = total + fx_recv[d, j].astype(F32)
        ybuf[j, PAD_W:ROWS, :] = total.astype(BF16)
        return carry

    lax.fori_loop(0, 16, fl_x_add, 0)

    def y_copy(d):
        to = lax.rem(yy + d, 4)
        src = ybuf.at[pl.ds(4 * to, 4)]
        return remote(src, y_recv.at[d - 1], y_s.at[d - 1], y_r.at[d - 1], (g, shard_at(to, zl, core)))

    for d in range(1, 4):
        y_copy(d).start()
    for d in range(1, 4):
        y_copy(d).wait()
    for j in range(4):
        total = ybuf[4 * yy + j].astype(F32)
        for d in range(3):
            total = total + y_recv[d, j].astype(F32)
        zbuf[j] = total.astype(BF16)

    def z_copy(d):
        to = lax.rem(zl + d, 4)
        return remote(zbuf.at[to], z_recv.at[d - 1], z_s.at[d - 1], z_r.at[d - 1], (g, shard_at(yy, to, core)))

    for d in range(1, 4):
        z_copy(d).start()
    for d in range(1, 4):
        z_copy(d).wait()
    total = zbuf[zl].astype(F32)
    for d in range(3):
        total = total + z_recv[d].astype(F32)
    h_send[...] = total.astype(BF16)

    far = remote(h_send, h_recv, h_s.at[0], h_r.at[0], (lax.rem(g + 4, 8), s))
    far.start()

    for d in range(1, GROUPS):
        mid_copy(d).wait()
    mid_total = mid_send[xx * 2 + zh].astype(F32)
    for d in range(GROUPS - 1):
        mid_total = mid_total + mid_recv[d].astype(F32)
    mout_ref[...] = mid_total

    far.wait()
    total = total + h_recv[...].astype(F32)
    total = jnp.where(zh == 0, total, pltpu.roll(total, 64, 1))
    wout_ref[...] = total[0:BLOCK_W, 0:64]
    fout_ref[...] = total[PAD_W:ROWS, 0:32]
    lout_ref[...] = total[PAD_W:ROWS, 32:64]

    sent = send_c.at[pl.ds(1, SHARDS - 1)]
    pltpu.make_async_copy(sent, sent, a_s.at[0]).wait()
    sent = recv_m.at[pl.ds(1, SHARDS - 1)]
    pltpu.make_async_copy(sent, sent, a_s.at[1]).wait()
    sent = send_h.at[pl.ds(1, SHARDS - 1)]
    pltpu.make_async_copy(sent, sent, a_s.at[2]).wait()


def body(
    top_input,
    pre_act,
    grad_hidden,
    top_weight,
    core_first,
    core_mid,
    core_last,
    bag_ids,
    lookup_order,
    hot_rows,
    cold_digits,
):
    s = lax.axis_index("shard")
    bags = bag_ids[0, 0]
    rowmap = bags % 26 * 128 + bags // 26
    order = lookup_order[0, 0]
    mine = (jnp.arange(4) == s % 4).astype(I32)
    hot = hot_rows[0, 0].reshape(SHARDS, 1, PER_HOT) * mine[None, :, None]
    digits = cold_digits[0, 0].reshape(3, SHARDS, 1, PER_COLD)
    digits = digits - (jnp.arange(3) == 1).astype(I32)[:, None, None, None] * (
        jnp.arange(SHARDS, dtype=I32)[None, :, None, None] * 32
    )
    digits = (digits * mine[None, None, :, None]).reshape(3, SHARDS, 128)
    meta = jnp.concatenate(
        [hot.reshape(SHARDS, 3, 128), digits.transpose(1, 0, 2), jnp.zeros((SHARDS, 2, 128), I32)], axis=1
    )
    block = lax.dynamic_slice_in_dim(core_mid, s * 32, 32, 0).reshape(8, 4, RANK, E2, RANK)
    midq = block.transpose(1, 3, 2, 0, 4).reshape(256, 256)
    midl = block.transpose(0, 4, 1, 3, 2).reshape(256, 256)

    vmem = pl.BlockSpec(memory_space=pltpu.VMEM)
    smem = pl.BlockSpec(memory_space=pltpu.SMEM)

    def buf(*shape, dtype=BF16):
        return pltpu.VMEM(shape, dtype)

    dma = pltpu.SemaphoreType.DMA
    outs = pl.pallas_call(
        kernel,
        out_shape=(
            jax.ShapeDtypeStruct((128, 128), BF16),
            jax.ShapeDtypeStruct((2048, 128), F32),
            jax.ShapeDtypeStruct((BLOCK_W, 64), F32),
            jax.ShapeDtypeStruct((32, 32), F32),
            jax.ShapeDtypeStruct((32, 32), F32),
            jax.ShapeDtypeStruct((32, 256), F32),
        ),
        in_specs=[vmem, vmem, vmem, vmem, smem, smem, vmem, vmem, vmem, vmem, vmem],
        out_specs=(vmem,) * 6,
        scratch_shapes=[
            buf(26 * 128, 128, dtype=F32),
            buf(PER_HOT, 128, dtype=F32),
            buf(SHARDS, PER_COLD, 128),
            buf(SHARDS, PER_HOT, 128),
            buf(SHARDS, PER_COLD, 128),
            buf(SHARDS, PER_HOT, 128),
            buf(SHARDS, 8, 128, dtype=I32),
            buf(2, 16, PAD_W, 128),
            buf(16, PAD_W, 128),
            buf(256, 512),
            buf(4, 16, PAD_W, 128),
            buf(2, 3, 8, PAD_W, 128),
            buf(256, 1024),
            buf(256, 1024),
            buf(1024, 2048),
            buf(256, 128, dtype=F32),
            buf(256, 128, dtype=F32),
            buf(128, 128, dtype=F32),
            buf(256, 1024),
            buf(256, 1024),
            buf(64, 1024, dtype=F32),
            buf(512, 1024),
            buf(512, 2048),
            buf(256, 256, dtype=F32),
            buf(8, 32, 256),
            buf(7, 32, 256),
            buf(2, 16, 32, 512, dtype=F32),
            buf(16, 32, 512),
            buf(16, 32, 512),
            buf(4, 16, 32, 128),
            buf(3, 16, 32, 128),
            buf(16, ROWS, 128),
            buf(3, 4, ROWS, 128),
            buf(4, ROWS, 128),
            buf(3, ROWS, 128),
            buf(ROWS, 128),
            buf(ROWS, 128),
            dma((3,)),
            dma((3,)),
            dma((3,)),
            dma((3,)),
            dma((2, 3)),
            dma((2, 3)),
            dma((3,)),
            dma((3,)),
            dma((3,)),
            dma((3,)),
            dma((3,)),
            dma((3,)),
            dma((1,)),
            dma((1,)),
            dma((7,)),
            dma((7,)),
        ],
        compiler_params=pltpu.CompilerParams(
            collective_id=0, has_side_effects=True, vmem_limit_bytes=56 * 1024 * 1024
        ),
    )(
        pre_act,
        grad_hidden,
        top_weight,
        top_input,
        rowmap,
        order,
        meta,
        core_first,
        core_last,
        midq,
        midl,
    )
    dense_grad, hot_grad, weight_grad, first_grad, last_grad, mid = outs
    mid_grad = mid.reshape(4, 4, E2, 8, RANK).transpose(3, 1, 0, 2, 4).reshape(32, 256)
    return (hot_grad[None], dense_grad, weight_grad, first_grad, mid_grad, last_grad)


def solution(mesh):
    return jax.shard_map(
        body,
        mesh=mesh,
        in_specs=(
            P(("group", "shard"), None),
            P(("group", "shard"), None),
            P(("group", "shard"), None),
            P(),
            P(),
            P(),
            P(),
            P("group", "shard", None),
            P("group", "shard", None),
            P("group", "shard", None),
            P("group", "shard", None, None),
        ),
        out_specs=(
            P("group", "shard", None),
            P(("group", "shard"), None),
            P("shard", "group"),
            P("shard", "group"),
            P("shard", "group"),
            P("shard", "group"),
        ),
        check_vma=False,
    )
```

time: 1220 us -> 107 us (0.09)
  waiting for transfers between devices: 986 us -> 0 us
  other arithmetic: 88 us -> 5.27 us
  Pallas kernels: 0 us -> 82.7 us
  local copies, waits for them, and re-layouts: 92.3 us -> 16.5 us
  matrix products: 18.8 us -> 0 us
  starting transfers between devices: 17.1 us -> 0 us
  between operations: 15.1 us -> 0.76 us
    reduce_scatter x5 -> x0, waiting for transfers between devices: 542 us -> none  [the longest x1 160 us: body(): lax.psum_scatter(local_sums[3], 'shard', scatter_dimension=0, tiled=True)]
    unnamed x11 -> x0, waiting for transfers between devices: 445 us -> none
    pallas_call x0 -> x1, Pallas kernels: none -> 82.7 us  [body(): pl.pallas_call(kernel, out_shape=(jax.ShapeDtypeStruct((128, 128), BF16),...]
    gather x8 -> x0, local copies, waits for them, and re-layouts: 69.8 us -> none  [the longest x2 30.8 us: body(): sent = pooled[bags[order[:HOT_N]]].reshape(shards, per_owner, E)]
    reduce_sum x5 -> x0, other arithmetic: 50.1 us -> none  [the longest x1 32.3 us: middle_terms(): jnp.sum(prod_h[:, :, None, :, :] * last_wide[None, None, :, :, :], axis=3)]
    dot_general x5 -> x0, matrix products: 18.8 us -> none  [the longest x3 12.6 us: by_digit(): lax.dot_general(onehot, terms_cols, (((1,), (1,)), ((), ())), preferred_e...]
    scatter-add x1 -> x0, other arithmetic: 18.3 us -> none  [body(): jax.ops.segment_sum(arrived.reshape(-1, E).astype(jnp.float32), arrived_r...]
    all_to_all x2 -> x0, starting transfers between devices: 16.7 us -> none  [the longest x1 8.93 us: body(): lax.all_to_all(targets, 'shard', split_axis=0, concat_axis=0, tiled=True)]
  transfers between devices with their start and end apart: 10 -> 0, of which waited for: 8 -> 0; matrix products, arithmetic and copies ran while one was open for 7% -> 0% of each run, Pallas kernels for 0% -> 0%
where the time goes in v1:
time: 107 us; the launch traced here: 105 us
  Pallas kernels  82.7 us (77%)
  local copies, waits for them, and re-layouts  16.5 us (15%)
  other arithmetic  5.27 us (5%)
    pallas_call x1, Pallas kernels, body(): pl.pallas_call(kernel, out_shape=(jax.ShapeDtypeStruct((128, 128), BF16),...  82.7 us
    unnamed x6, local copies, waits for them, and re-layouts  8.31 us

profile of v1, /device:TPU:6, one launch (start us, length us, event | category | flops | bytes accessed | tf_op | source)
XLA Modules:
  0.0 105.2 jit_solution(9744849778678489630)
XLA Ops:
  1.1 0.8 compare_reduce_fusion
  1.9 0.5 broadcast.76
  2.4 1.4 %reduce.6 = s32[3072]{0:T(1024)S(1)} reduce(s32[1,1,3072]{2,1,0:T(1,128)} %param.20, s32[]{:T(128)} %broadcast.76), dimensions={0,1}, to_apply=%param.20.reduce_sub_computation.3 | reduce | bytes 24580 | tf_op args[9]
  3.9 0.7 reduce.2
  4.6 0.1 reshape_squeeze.4
  4.8 0.8 broadcast_divide_fusion
  5.6 0.6 fusion.2.rowmap
  6.2 0.1 mul.84
  6.4 0.9 constant_dynamic-slice_fusion
  7.3 0.1 mul.95
  7.5 0.7 add_add_fusion.meta_ref
  8.2 0.4 reshape.102
  8.6 0.3 copy.28
  9.0 1.0 reshape.103.midq_ref
  10.0 2.0 %copy.29 = bf16[8,32,4,2,32]{4,3,2,1,0:T(2,128)(2,1)S(1)} copy(bf16[8,32,4,2,32]{1,3,4,2,0:T(2,128)(2,1)S(1)} %bitcast.12) | data formatting | bytes 262144 | tf_op jit(solution)/shard_map/transpose | solution.py:452
  12.0 1.0 reshape.104.midl_ref
  13.0 82.7 %shard_map.154 = (bf16[128,128]{1,0:T(8,128)(2,1)}, f32[2048,128]{1,0:T(8,128)}, f32[108,64]{1,0:T(8,128)}, f32[32,32]{1,0:T(8,128)}, f32[32,32]{1,0:T(8,128)}, /*index=5*/f32[32,256]{1,0:T(8,128)}) custom-call(bf16[128,512]{1,0:T(8,128)(2,1)} %act_ref.1, bf16[128,512]{1,0:T(8,128)(2,1)} %hid_ref.1, bf16[3456,512]{1,0:T(8,128)(2,1)} %tw_ref.1, ...), custom_call_target="tpu_custom_call" | custom-call | tf_op jit(solution)/shard_map/pallas_call | solution.py:461
  95.7 1.5 %copy.31 = f32[108,64]{0,1:T(8,128)} copy(f32[108,64]{1,0:T(8,128)} %get-tuple-element.32) | data formatting | bytes 55296
  97.2 0.8 reshape.105
  98.2 0.8 reshape.106
  98.9 2.3 %copy.39 = f32[1,2048,128]{2,1,0:T(8,128)} copy(f32[1,2048,128]{2,1,0:T(8,128)} %bitcast.13) | data formatting | bytes 2097152
  101.2 1.4 %copy.40 = bf16[128,128]{1,0:T(8,128)(2,1)} copy(bf16[128,128]{1,0:T(8,128)(2,1)} %get-tuple-element.45) | data formatting | bytes 65536
  102.6 1.3 %copy.41 = f32[32,32]{1,0:T(8,128)} copy(f32[32,32]{1,0:T(8,128)} %get-tuple-element.47) | data formatting | bytes 8192
  103.9 1.3 %copy.42 = f32[32,32]{1,0:T(8,128)} copy(f32[32,32]{1,0:T(8,128)} %get-tuple-element.49) | data formatting | bytes 8192
  (17 shorter events, 0.8 us)

commit v2 on v1

v2 whole, which is shorter than its diff:
```python
import functools

import jax
import jax.numpy as jnp
from jax import lax
from jax.experimental import pallas as pl
from jax.experimental.pallas import tpu as pltpu
from jax.sharding import PartitionSpec as P

F32 = jnp.float32
BF16 = jnp.bfloat16
I32 = jnp.int32

E = 128
RANK = 32
E1 = 8
E2 = 2
E3 = 8
HOT_N = 3072
SHARDS = 32
GROUPS = 8
PER_HOT = 96
PER_COLD = 32
BLOCK_W = 108
PAD_W = 112
ROWS = PAD_W + 32
MESH = pl.DeviceIdType.MESH


def iota(shape, dim):
    return lax.broadcasted_iota(I32, shape, dim)


def dot(a, b):
    return jnp.dot(a, b, preferred_element_type=F32)


def dot_nt(a, b):
    return lax.dot_general(a, b, (((1,), (1,)), ((), ())), preferred_element_type=F32)


def zero_one(mask):
    return jnp.where(mask, 1.0, 0.0).astype(BF16)


def kernel(
    act_hbm, hid_hbm, tw_hbm, x_hbm, bags, order, hot_in, dig_in, first_hbm, last_hbm, midq_ref,
    dense_ref, hot_hbm, wout_ref, fout_ref, lout_ref, mout_ref,
    act_ref, hid_ref, tw_ref, x_ref, first_ref, last_ref, midl, hot,
    pooled, stage, meta, send_c, send_h, recv_c, recv_h, recv_m,
    xt, xt_recv, pre2, w_own, ring,
    first_t, last_t, onehot, a_t, c_t, q_t, he, ce, qs, tf, tl, mid_acc, mid_send, mid_recv,
    fl_own, fl_send, fl_recv, fx, fx_recv,
    wy, wy_recv, wz, wz_recv, fy, fy_recv, fz, fz_recv,
    load_s, core_s, core_r, a_s, a_r, ring_s, ring_r, f_s, f_r, wy_s, wy_r, wz_s, wz_r,
    fy_s, fy_r, fz_s, fz_r, m_s, m_r,
):
    g = lax.axis_index("group")
    s = lax.axis_index("shard")
    xx = lax.rem(g, 4)
    zh = g // 4
    core = lax.rem(s, 2)
    zl = lax.rem(s // 2, 4)
    yy = s // 8
    deep = zh * 4 + zl

    load_act = pltpu.make_async_copy(act_hbm, act_ref, load_s.at[0])
    load_hid = pltpu.make_async_copy(hid_hbm, hid_ref, load_s.at[1])
    load_x = pltpu.make_async_copy(x_hbm, x_ref, load_s.at[2])
    load_tw = pltpu.make_async_copy(tw_hbm, tw_ref, load_s.at[3])
    load_first = pltpu.make_async_copy(first_hbm, first_ref, load_s.at[4])
    load_last = pltpu.make_async_copy(last_hbm, last_ref, load_s.at[5])
    load_act.start()
    load_hid.start()
    load_x.start()
    load_tw.start()
    load_first.start()
    load_last.start()

    def shard_at(y, z, c):
        return y * 8 + z * 2 + c

    def remote(src, dst, send_sem, recv_sem, to):
        return pltpu.make_async_remote_copy(
            src_ref=src, dst_ref=dst, send_sem=send_sem, recv_sem=recv_sem, device_id=to, device_id_type=MESH
        )

    def along_z(d):
        to = lax.rem(deep + d, 8)
        return to, ((to // 4) * 4 + xx, shard_at(yy, lax.rem(to, 4), core))

    partner = (g, shard_at(yy, zl, 1 - core))

    barrier = pltpu.get_barrier_semaphore()

    def greet_shard(k, carry):
        pl.semaphore_signal(barrier, inc=1, device_id=(g, lax.rem(s + k, SHARDS)), device_id_type=MESH)
        return carry

    def greet_group(k, carry):
        pl.semaphore_signal(barrier, inc=1, device_id=(lax.rem(g + k, GROUPS), s), device_id_type=MESH)
        return carry

    def greet_far(k, carry):
        to = (lax.rem(g + 4, 8), shard_at(yy, lax.rem(zl + k, 4), core))
        pl.semaphore_signal(barrier, inc=1, device_id=to, device_id_type=MESH)
        return carry

    lax.fori_loop(1, SHARDS, greet_shard, 0)
    lax.fori_loop(1, GROUPS, greet_group, 0)
    lax.fori_loop(1, 4, greet_far, 0)

    meta[...] = jnp.zeros_like(meta)
    mine = lax.rem(s, 4)
    hots = jnp.concatenate([hot_in[pl.ds(c, 8, stride=3), :] for c in range(3)], axis=1)

    def place(values, width, i):
        lane = iota(values.shape, 1)
        kept = jnp.where((lane >= i * width) & (lane < (i + 1) * width), values, 0)
        out = kept
        for j in range(4):
            if j != i:
                out = jnp.where(mine == j, pltpu.roll(kept, (j - i) % 4 * width, 1), out)
        return out

    for i in range(4):
        out = place(hots, PER_HOT, i)
        for q in range(8):
            for c in range(3):
                meta[4 * q + i, c : c + 1, :] = out[q : q + 1, c * 128 : (c + 1) * 128]
    for r in range(3):
        digit = dig_in[0, 0, r : r + 1, :]
        if r == 1:
            digit = digit % 32
        digit = jnp.concatenate([digit[:, q * 128 : (q + 1) * 128] for q in range(8)], axis=0)
        for i in range(4):
            out = place(digit, PER_COLD, i)
            for q in range(8):
                meta[4 * q + i, 3 + r : 4 + r, :] = out[q : q + 1, :]

    load_act.wait()
    load_hid.wait()
    pre = jnp.where(act_ref[...].astype(F32) > 0, hid_ref[...].astype(F32), 0.0).astype(BF16)
    col = iota((512, 512), 1)
    source = (col // 64 % 2) * 256 + (col // 128) * 64 + col % 64
    pre2[0:128, :] = dot(pre, zero_one(iota((512, 512), 0) == source)).astype(BF16)

    load_x.wait()
    for shard in range(SHARDS):
        lo = shard * BLOCK_W // 128 * 128
        off = shard * BLOCK_W - lo
        width = 128 if off + BLOCK_W <= 128 else 256
        pick = zero_one(iota((PAD_W, width), 1) == iota((PAD_W, width), 0) + off)
        xt[shard % 2, shard // 2] = dot_nt(pick, x_ref[:, lo : lo + width]).astype(BF16)

    pl.semaphore_wait(barrier, SHARDS - 1 + GROUPS - 1 + 3)
    send_pre = remote(pre2.at[0:128], pre2.at[128:256], core_s.at[0], core_r.at[0], partner)
    send_pre.start()
    send_xt = remote(xt.at[1 - core], xt_recv, core_s.at[1], core_r.at[1], partner)
    send_xt.start()

    load_tw.wait()
    dense_ref[...] = dot_nt(pre, tw_ref[0:128, :]).astype(BF16)
    for i in range(13):
        part = dot_nt(pre, tw_ref[128 + i * 256 : 384 + i * 256, :]).astype(BF16).astype(F32)
        pooled[pl.ds(2 * i, 128, stride=26), :] = part[:, 0:128]
        pooled[pl.ds(2 * i + 1, 128, stride=26), :] = part[:, 128:256]

    def gather(base, count):
        for j in range(count):
            r = bags[0, 0, order[0, 0, base + j]]
            stage[pl.ds(j, 1), :] = pooled[pl.ds(r, 1), :]
        return stage[0:count, :].astype(BF16)

    def cold_to(k, carry):
        o = lax.rem(s + k, SHARDS)
        send_c[k] = gather(HOT_N + o * PER_COLD, PER_COLD)
        remote(send_c.at[k], recv_c.at[s], a_s.at[0], a_r.at[0], (g, o)).start()
        remote(meta.at[o], recv_m.at[s], a_s.at[1], a_r.at[1], (g, o)).start()
        return carry

    def hot_to(k, carry):
        o = lax.rem(s + k, SHARDS)
        send_h[k] = gather(o * PER_HOT, PER_HOT)
        remote(send_h.at[k], recv_h.at[s], a_s.at[2], a_r.at[2], (g, o)).start()
        return carry

    lax.fori_loop(1, SHARDS, cold_to, 0)
    send_c[0] = gather(HOT_N + s * PER_COLD, PER_COLD)
    pltpu.make_async_copy(send_c.at[0], recv_c.at[s], a_r.at[0]).start()
    pltpu.make_async_copy(meta.at[s], recv_m.at[s], a_r.at[1]).start()

    send_pre.wait()
    send_xt.wait()
    pre_both = pre2[...]
    for j in range(0, 16, 4):
        both = jnp.concatenate(
            [xt[core, j : j + 4].reshape(4 * PAD_W, 128), xt_recv[j : j + 4].reshape(4 * PAD_W, 128)], axis=1
        )
        part = dot(both, pre_both).astype(BF16)
        for k in range(4):
            w_own[k, j : j + 4] = part[:, k * 128 : (k + 1) * 128].reshape(4, PAD_W, 128)

    right = (zh * 4 + lax.rem(xx + 1, 4), s)
    left = (zh * 4 + lax.rem(xx + 3, 4), s)

    def ring_copy(way, step):
        to = right if way == 0 else left
        if step == 0:
            chunk = lax.rem(xx + 3, 4) if way == 0 else lax.rem(xx + 1, 4)
            src = w_own.at[chunk, pl.ds(way * 8, 8)]
        else:
            src = ring.at[way, step - 1]
        return remote(src, ring.at[way, step], ring_s.at[way, step], ring_r.at[way, step], to)

    def ring_add(way, step):
        chunk = lax.rem(xx + 2 - step, 4) if way == 0 else lax.rem(xx + 2 + step, 4)

        def add(j, carry):
            total = ring[way, step, j].astype(F32) + w_own[chunk, way * 8 + j].astype(F32)
            ring[way, step, j] = total.astype(BF16)
            return carry

        lax.fori_loop(0, 8, add, 0)

    def ring_next(step):
        for way in range(2):
            ring_copy(way, step - 1).wait()
            ring_add(way, step - 1)
            ring_copy(way, step).start()

    for way in range(2):
        ring_copy(way, 0).start()

    lax.fori_loop(1, SHARDS, hot_to, 0)
    send_h[0] = gather(s * PER_HOT, PER_HOT)
    pltpu.make_async_copy(send_h.at[0], recv_h.at[s], a_r.at[2]).start()

    load_first.wait()
    load_last.wait()
    eye = zero_one(iota((256, 256), 0) == iota((256, 256), 1))
    first_t[...] = dot_nt(eye, first_ref[...]).astype(BF16)
    turn_row = iota((256, 256), 0)
    turn = zero_one(iota((256, 256), 1) == (turn_row % 32) * 8 + turn_row // 32)
    last_t[...] = dot_nt(turn, last_ref[...]).astype(BF16)
    midl[...] = dot_nt(eye, midq_ref[...]).astype(BF16)
    mid_acc[...] = jnp.zeros_like(mid_acc)

    ring_next(1)

    pltpu.make_async_copy(recv_c, recv_c, a_r.at[0]).wait()
    pltpu.make_async_copy(recv_m, recv_m, a_r.at[1]).wait()

    def digits(t, row):
        four = recv_m[pl.ds(4 * t, 4), row : row + 1, :]
        return four[0] + four[1] + four[2] + four[3]

    def pick_cores(u, carry):
        lanes = pl.ds(pl.multiple_of(u * 256, 256), 256)
        for i, (table, out) in enumerate(((first_t, a_t), (last_t, c_t))):
            digit = jnp.concatenate([digits(2 * u, 3 + 2 * i), digits(2 * u + 1, 3 + 2 * i)], axis=1)
            for k in range(4):
                row = iota((256, 256), 0) + k * 256
                onehot[i, k * 256 : (k + 1) * 256, lanes] = zero_one(row == digit)
            part = dot(table[...], onehot[i, :, lanes])
            out[2 * u] = part[:, 0:128]
            out[2 * u + 1] = part[:, 128:256]
        return carry

    lax.fori_loop(0, 4, pick_cores, 0)

    def cold_tile(t, carry):
        lanes = pl.ds(pl.multiple_of(t * 128, 128), 128)
        two = digits(t, 4)
        q_t[...] = recv_c[pl.ds(4 * t, 4)].reshape(128, 128).astype(F32).T
        low = jnp.broadcast_to(jnp.concatenate([two % 4, two % 4], axis=1), (8, 256))
        high = jnp.broadcast_to(jnp.concatenate([two // 4, two // 4], axis=1), (8, 256))
        is_low = [low == k for k in range(4)]
        is_high = [high == k for k in range(8)]

        def packed(mask):
            half = jnp.where(mask, 1.0, 0.0)
            return jnp.concatenate([half, half], axis=0).astype(BF16)

        keep_low = [packed(m) for m in is_low]
        keep_high = [packed(m) for m in is_high]
        for pair in range(4):
            cols = slice(pair * 256, (pair + 1) * 256)
            for e2 in range(2):
                halves = []
                for e3 in (2 * pair, 2 * pair + 1):
                    total = None
                    for e1 in range(8):
                        q_row = e1 * 16 + e2 * 8 + e3
                        term = a_t[t, e1 * 32 : (e1 + 1) * 32, :] * q_t[q_row : q_row + 1, :]
                        total = term if total is None else total + term
                    halves.append(total)
                h = jnp.concatenate(halves, axis=1).astype(BF16).reshape(2, 16, 256)
                for k in range(4):
                    he[k * 64 + e2 * 32 : k * 64 + e2 * 32 + 32, cols] = (h * keep_low[k][None]).reshape(32, 256)
            c = jnp.concatenate(
                [c_t[t, e3 * 32 : (e3 + 1) * 32, :] for e3 in (2 * pair, 2 * pair + 1)], axis=1
            )
            c = c.astype(BF16).reshape(2, 16, 256)
            for k in range(8):
                ce[k * 32 : (k + 1) * 32, cols] = (c * keep_high[k][None]).reshape(32, 256)
            q_all = dot(midq_ref[...], ce[:, cols]).reshape(4, 8, 8, 256)
            total = q_all[0]
            for k in range(1, 4):
                total = jnp.where(is_low[k][None], q_all[k], total)
            qs[:, cols] = total.reshape(64, 256)
            l_all = dot(midl[...], he[:, cols]).reshape(8, 4, 8, 256)
            total = l_all[0]
            for k in range(1, 8):
                total = jnp.where(is_high[k][None], l_all[k], total)
            total = total.reshape(32, 256).astype(BF16)
            tl[pair * 64 : pair * 64 + 32, lanes] = total[:, 0:128]
            tl[pair * 64 + 32 : pair * 64 + 64, lanes] = total[:, 128:256]
        mid_acc[...] += dot_nt(he[...], ce[...])
        for e1 in range(8):
            total = None
            for e2 in range(2):
                for e3 in range(8):
                    q_row = e1 * 16 + e2 * 8 + e3
                    term = qs[e2 * 32 : (e2 + 1) * 32, e3 * 128 : (e3 + 1) * 128] * q_t[q_row : q_row + 1, :]
                    total = term if total is None else total + term
            row = (e1 % 4) * 64 + (e1 // 4) * 32
            tf[row : row + 32, lanes] = total.astype(BF16)
        return carry

    lax.fori_loop(0, 4, cold_tile, 0)
    ring_next(2)
    lax.fori_loop(4, 8, cold_tile, 0)

    row = iota((256, 256), 0)
    j = row % 32
    source = (j % 8) * 32 + ((row // 32 % 2) * 4 + row // 64) * 4 + j // 8
    tl[...] = dot(zero_one(iota((256, 256), 1) == source), tl[...]).astype(BF16)
    lane = iota((256, 128), 1)

    def by_digit(k, carry):
        rows = pl.ds(pl.multiple_of(k * 256, 256), 256)
        one = dot_nt(onehot[0, rows, :], tf[...])
        two = dot_nt(onehot[1, rows, :], tl[...])
        for i in range(4):
            a = one[:, i // 2 * 128 : i // 2 * 128 + 128]
            b = two[:, i // 2 * 128 : i // 2 * 128 + 128]
            if i % 2 == 0:
                part = jnp.where(lane < 64, a, pltpu.roll(b, 64, 1))
            else:
                part = jnp.where(lane < 64, pltpu.roll(a, 64, 1), b)
            for n in range(8):
                fl_own[n % 2, i, 4 * k + n // 2] = part[n * 32 : (n + 1) * 32, :]
        return carry

    lax.fori_loop(0, 4, by_digit, 0)

    def fl_round(j, carry):
        for i in range(4):
            fl_send[i, j] = fl_own[1 - core, i, j].astype(BF16)
        return carry

    lax.fori_loop(0, 16, fl_round, 0)
    fl_copy = remote(fl_send, fl_recv, core_s.at[2], core_r.at[2], partner)
    fl_copy.start()

    row = iota((256, 256), 0)
    source = (row % 4) * 64 + (row // 4 % 2) * 32 + ((row // 32 % 2) * 4 + row // 64) * 4 + row // 8 % 4
    moved = dot(zero_one(iota((256, 256), 1) == source), mid_acc[...].astype(BF16)).astype(BF16)
    for k in range(8):
        mid_send[k] = moved[k * 32 : (k + 1) * 32, :]

    def mid_copy(d):
        to = lax.rem(g + d, GROUPS)
        src = mid_send.at[lax.rem(to, 4) * 2 + to // 4]
        return remote(src, mid_recv.at[d - 1], m_s.at[d - 1], m_r.at[d - 1], (to, s))

    for d in range(1, GROUPS):
        mid_copy(d).start()

    for way in range(2):
        ring_copy(way, 2).wait()

        def last_add(j, carry):
            total = ring[way, 2, j].astype(F32) + w_own[xx, way * 8 + j].astype(F32)
            wy[way * 8 + j] = total.astype(BF16)
            return carry

        lax.fori_loop(0, 8, last_add, 0)

    def y_copy(buf, into, send_sem, recv_sem, d):
        to = lax.rem(yy + d, 4)
        src = buf.at[pl.ds(4 * to, 4)]
        return remote(src, into.at[d - 1], send_sem.at[d - 1], recv_sem.at[d - 1], (g, shard_at(to, zl, core)))

    for d in range(1, 4):
        y_copy(wy, wy_recv, wy_s, wy_r, d).start()

    fl_copy.wait()

    def fl_pair(j, carry):
        for i in range(4):
            fx[i, j] = (fl_own[core, i, j] + fl_recv[i, j].astype(F32)).astype(BF16)
        return carry

    lax.fori_loop(0, 16, fl_pair, 0)

    def fl_x(d):
        to = lax.rem(xx + d, 4)
        return remote(fx.at[to], fx_recv.at[d - 1], f_s.at[d - 1], f_r.at[d - 1], (zh * 4 + to, s))

    for d in range(1, 4):
        fl_x(d).start()

    pltpu.make_async_copy(recv_h, recv_h, a_r.at[2]).wait()
    hot[...] = jnp.zeros_like(hot)

    def hot_part(i, carry):
        ids = []
        for half in range(2):
            four = recv_m[pl.ds(8 * i + 4 * half, 4), :, :]
            four = four[0] + four[1] + four[2] + four[3]
            ids += [four[k : k + 1, :] for k in range(3)]
        values = recv_h[pl.ds(8 * i, 8)].reshape(768, 128).astype(F32)
        low = jnp.concatenate(ids, axis=1) % 512
        pick = zero_one(iota((512, 768), 0) == low)
        column = jnp.concatenate(
            [jnp.broadcast_to((r // 512).astype(F32), (128, 128)).T for r in ids], axis=0
        )
        for k in range(0, 4, 2):
            both = [jnp.where(column == float(k + n), values, 0.0).astype(BF16) for n in range(2)]
            part = dot(pick, jnp.concatenate(both, axis=1))
            hot[k * 512 : (k + 1) * 512, :] += part[:, 0:128]
            hot[(k + 1) * 512 : (k + 2) * 512, :] += part[:, 128:256]
        return carry

    lax.fori_loop(0, 4, hot_part, 0)
    save_hot = pltpu.make_async_copy(hot, hot_hbm, load_s.at[6])
    save_hot.start()

    for d in range(1, 4):
        fl_x(d).wait()

    def fl_x_add(j, carry):
        total = fx[xx, j].astype(F32)
        for d in range(3):
            total = total + fx_recv[d, j].astype(F32)
        fy[j] = total.astype(BF16)
        return carry

    lax.fori_loop(0, 16, fl_x_add, 0)
    for d in range(1, 4):
        y_copy(fy, fy_recv, fy_s, fy_r, d).start()

    for d in range(1, 4):
        y_copy(wy, wy_recv, wy_s, wy_r, d).wait()

    def halves(total, count, width):
        top, bottom = total[0:count], total[count : 2 * count]
        left_half = iota((count, 128), 1) % (2 * width) < width
        return (
            jnp.where(left_half, top, pltpu.roll(bottom, width, 1)),
            jnp.where(left_half, pltpu.roll(top, 128 - width, 1), bottom),
        )

    def z_copy(buf, into, send_sem, recv_sem, d):
        to, device = along_z(d)
        return remote(buf.at[to], into.at[d - 1], send_sem.at[d - 1], recv_sem.at[d - 1], device)

    for j in range(4):
        total = wy[4 * yy + j].astype(F32)
        for d in range(3):
            total = total + wy_recv[d, j].astype(F32)
        for k, half in enumerate(halves(total, 56, 64)):
            wz[4 * k + j] = jnp.concatenate([half, jnp.zeros((8, 128), F32)], axis=0).astype(BF16)
    for d in range(1, 8):
        z_copy(wz, wz_recv, wz_s, wz_r, d).start()

    for d in range(1, 4):
        y_copy(fy, fy_recv, fy_s, fy_r, d).wait()
    for j in range(4):
        total = fy[4 * yy + j].astype(F32)
        for d in range(3):
            total = total + fy_recv[d, j].astype(F32)
        for k, half in enumerate(halves(total, 16, 32)):
            fz[4 * k + j] = half.astype(BF16)
    for d in range(1, 8):
        z_copy(fz, fz_recv, fz_s, fz_r, d).start()

    for d in range(1, GROUPS):
        mid_copy(d).wait()
    total = mid_send[xx * 2 + zh].astype(F32)
    for d in range(GROUPS - 1):
        total = total + mid_recv[d].astype(F32)
    mout_ref[...] = total

    for d in range(1, 8):
        z_copy(wz, wz_recv, wz_s, wz_r, d).wait()
    total = wz[deep].astype(F32)
    for d in range(7):
        total = total + wz_recv[d].astype(F32)
    wout_ref[0:56, :] = total[0:56, 0:64]
    wout_ref[56:BLOCK_W, :] = pltpu.roll(total, 64, 1)[0 : BLOCK_W - 56, 0:64]

    for d in range(1, 8):
        z_copy(fz, fz_recv, fz_s, fz_r, d).wait()
    total = fz[deep].astype(F32)
    for d in range(7):
        total = total + fz_recv[d].astype(F32)
    fout_ref[0:16, :] = total[:, 0:32]
    fout_ref[16:32, :] = pltpu.roll(total, 96, 1)[:, 0:32]
    lout_ref[0:16, :] = pltpu.roll(total, 64, 1)[:, 0:32]
    lout_ref[16:32, :] = pltpu.roll(total, 32, 1)[:, 0:32]

    save_hot.wait()
    sent = send_c.at[pl.ds(1, SHARDS - 1)]
    pltpu.make_async_copy(sent, sent, a_s.at[0]).wait()
    sent = recv_m.at[pl.ds(1, SHARDS - 1)]
    pltpu.make_async_copy(sent, sent, a_s.at[1]).wait()
    sent = send_h.at[pl.ds(1, SHARDS - 1)]
    pltpu.make_async_copy(sent, sent, a_s.at[2]).wait()


def finish(dense, hot, weight, first, last, mid, dense_out, hot_out, weight_out, first_out, last_out, mid_out):
    dense_out[...] = dense[...]
    hot_out[...] = hot[...]
    weight_out[...] = weight[...]
    first_out[...] = first[...]
    last_out[...] = last[...]
    for m1 in range(8):
        parts = []
        for a in range(4):
            for e2 in range(2):
                row = a * 8 + e2 * 4
                parts.append(mid[row : row + 4, m1 * 32 : (m1 + 1) * 32])
        mid_out[m1 * 4 : (m1 + 1) * 4, :] = jnp.concatenate(parts, axis=1)


def body(
    top_input,
    pre_act,
    grad_hidden,
    top_weight,
    core_first,
    core_mid,
    core_last,
    bag_ids,
    lookup_order,
    hot_rows,
    cold_digits,
):
    s = lax.axis_index("shard")
    block = lax.dynamic_slice_in_dim(core_mid, s * 32, 32, 0).reshape(8, 4, RANK, E2, RANK)
    midq = block.transpose(1, 3, 2, 0, 4).reshape(256, 256)

    vmem = pl.BlockSpec(memory_space=pltpu.VMEM)
    smem = pl.BlockSpec(memory_space=pltpu.SMEM)
    hbm = pl.BlockSpec(memory_space=pl.ANY)

    def buf(*shape, dtype=BF16):
        return pltpu.VMEM(shape, dtype)

    dma = pltpu.SemaphoreType.DMA
    shapes = (
        jax.ShapeDtypeStruct((128, 128), BF16),
        jax.ShapeDtypeStruct((2048, 128), F32),
        jax.ShapeDtypeStruct((BLOCK_W, 64), F32),
        jax.ShapeDtypeStruct((32, 32), F32),
        jax.ShapeDtypeStruct((32, 32), F32),
        jax.ShapeDtypeStruct((32, 256), F32),
    )
    outs = pl.pallas_call(
        kernel,
        out_shape=shapes,
        in_specs=[hbm, hbm, hbm, hbm, smem, smem, vmem, vmem, hbm, hbm, vmem],
        out_specs=(vmem, hbm, vmem, vmem, vmem, vmem),
        scratch_shapes=[
            buf(128, 512),
            buf(128, 512),
            buf(3456, 512),
            buf(128, 3456),
            buf(1024, 256),
            buf(1024, 256),
            buf(256, 256),
            buf(2048, 128, dtype=F32),
            buf(26 * 128, 128, dtype=F32),
            buf(PER_HOT, 128, dtype=F32),
            buf(SHARDS, 8, 128, dtype=I32),
            buf(SHARDS, PER_COLD, 128),
            buf(SHARDS, PER_HOT, 128),
            buf(SHARDS, PER_COLD, 128),
            buf(SHARDS, PER_HOT, 128),
            buf(SHARDS, 8, 128, dtype=I32),
            buf(2, 16, PAD_W, 128),
            buf(16, PAD_W, 128),
            buf(256, 512),
            buf(4, 16, PAD_W, 128),
            buf(2, 3, 8, PAD_W, 128),
            buf(256, 1024),
            buf(256, 1024),
            buf(2, 1024, 1024),
            buf(8, 256, 128, dtype=F32),
            buf(8, 256, 128, dtype=F32),
            buf(128, 128, dtype=F32),
            buf(256, 1024),
            buf(256, 1024),
            buf(64, 1024, dtype=F32),
            buf(256, 1024),
            buf(256, 1024),
            buf(256, 256, dtype=F32),
            buf(8, 32, 256),
            buf(7, 32, 256),
            buf(2, 4, 16, 32, 128, dtype=F32),
            buf(4, 16, 32, 128),
            buf(4, 16, 32, 128),
            buf(4, 16, 32, 128),
            buf(3, 16, 32, 128),
            buf(16, PAD_W, 128),
            buf(3, 4, PAD_W, 128),
            buf(8, 64, 128),
            buf(7, 64, 128),
            buf(16, 32, 128),
            buf(3, 4, 32, 128),
            buf(8, 16, 128),
            buf(7, 16, 128),
            dma((7,)),
            dma((3,)),
            dma((3,)),
            dma((3,)),
            dma((3,)),
            dma((2, 3)),
            dma((2, 3)),
            dma((3,)),
            dma((3,)),
            dma((3,)),
            dma((3,)),
            dma((7,)),
            dma((7,)),
            dma((3,)),
            dma((3,)),
            dma((7,)),
            dma((7,)),
            dma((7,)),
            dma((7,)),
        ],
        compiler_params=pltpu.CompilerParams(
            collective_id=0, has_side_effects=True, vmem_limit_bytes=56 * 1024 * 1024
        ),
    )(
        pre_act,
        grad_hidden,
        top_weight,
        top_input,
        bag_ids,
        lookup_order,
        hot_rows.reshape(24, 128),
        cold_digits,
        core_first,
        core_last,
        midq,
    )
    dense_grad, hot_grad, weight_grad, first_grad, last_grad, mid_grad = pl.pallas_call(
        finish,
        out_shape=shapes,
        in_specs=[vmem] * 6,
        out_specs=(vmem,) * 6,
    )(*outs)
    return (hot_grad[None], dense_grad, weight_grad, first_grad, mid_grad, last_grad)


def solution(mesh):
    return jax.shard_map(
        body,
        mesh=mesh,
        in_specs=(
            P(("group", "shard"), None),
            P(("group", "shard"), None),
            P(("group", "shard"), None),
            P(),
            P(),
            P(),
            P(),
            P("group", "shard", None),
            P("group", "shard", None),
            P("group", "shard", None),
            P("group", "shard", None, None),
        ),
        out_specs=(
            P("group", "shard", None),
            P(("group", "shard"), None),
            P("shard", "group"),
            P("shard", "group"),
            P("shard", "group"),
            P("shard", "group"),
        ),
        check_vma=False,
    )
```

time: 107 us -> 69.2 us (0.65); the launches traced: 105 us -> 68.7 us
  Pallas kernels: 82.7 us -> 62.6 us
  local copies, waits for them, and re-layouts: 16.5 us -> 5.48 us
  other arithmetic: 5.27 us -> 0 us
    pallas_call x1 -> x2, Pallas kernels: 82.7 us -> 62.6 us  [the longest x1 60.2 us: body(): pl.pallas_call(kernel, out_shape=shapes, in_specs=[hbm, hbm, hbm, hbm, sm...]
    unnamed x6 -> x2, local copies, waits for them, and re-layouts: 8.31 us -> 2.83 us
    reshape x3 -> x0, local copies, waits for them, and re-layouts: 2.65 us -> none  [the longest x2 1.63 us: body(): mid.reshape(4, 4, E2, 8, RANK).transpose(3, 1, 0, 2, 4).reshape(32, 256)]
    unnamed x2 -> x0, other arithmetic: 2.13 us -> none
    transpose x2 -> x0, local copies, waits for them, and re-layouts: 2.03 us -> none  [the longest x1 1.96 us: body(): midl = block.transpose(0, 4, 1, 3, 2).reshape(256, 256)]
where the time goes in v2:
time: 69.2 us; the launch traced here: 68.7 us
  Pallas kernels  62.6 us (90%)
  local copies, waits for them, and re-layouts  5.48 us (8%)
    pallas_call x1, Pallas kernels, body(): pl.pallas_call(kernel, out_shape=shapes, in_specs=[hbm, hbm, hbm, hbm, sm...  60.2 us
    unnamed x2, local copies, waits for them, and re-layouts  2.83 us
    pallas_call x1, Pallas kernels, body(): pl.pallas_call(finish, out_shape=shapes, in_specs=[vmem] * 6, out_specs=(...  2.32 us

profile of v2, /device:TPU:6, one launch (start us, length us, event | category | flops | bytes accessed | tf_op | source)
XLA Modules:
  0.0 68.7 jit_solution(2327430682565669529)
XLA Ops:
  0.6 1.3 %copy.20.dig_in = s32[1,1,3,1024]{3,2,1,0:T(4,128)} copy(s32[1,1,3,1024]{3,1,2,0:T(1,128)} %param.21) | data formatting | bytes 24576 | tf_op args[10]
  2.0 0.9 %constant_dynamic-slice_fusion = bf16[32,2048]{1,0:T(8,128)(2,1)S(1)} fusion(bf16[1024,2048]{1,0:T(8,128)(2,1)} %param.16, s32[]{:T(128)S(6)} %select_n.3), kind=kLoop, calls=%fused_computation | loop fusion | bytes 262148 | tf_op jit(solution)/shard_map/dynamic_slice | solution.py:553
  2.9 0.4 reshape.22
  3.2 0.3 copy.19
  3.6 1.0 %reshape.23.midq_ref = bf16[256,256]{1,0:T(8,128)(2,1)} reshape(bf16[4,2,32,8,32]{4,3,2,1,0:T(8,128)(2,1)S(1)} %copy.19) | data formatting | bytes 262144 | tf_op jit(solution)/shard_map/reshape | solution.py:554
  4.6 60.2 %shard_map.154 = (bf16[128,128]{1,0:T(8,128)(2,1)}, f32[2048,128]{1,0:T(8,128)}, f32[108,64]{1,0:T(8,128)}, f32[32,32]{1,0:T(8,128)}, f32[32,32]{1,0:T(8,128)}, /*index=5*/f32[32,256]{1,0:T(8,128)}) custom-call(bf16[128,512]{1,0:T(8,128)(2,1)} %act_hbm.1, bf16[128,512]{1,0:T(8,128)(2,1)} %hid_hbm.1, bf16[3456,512]{1,0:T(8,128)(2,1)} %tw_hbm.1, ...), custom_call_target="tpu_custom_call" | custom-call | tf_op jit(solution)/shard_map/pallas_call | solution.py:572
  64.9 2.3 %shard_map.155 = (bf16[128,128]{1,0:T(8,128)(2,1)}, f32[2048,128]{1,0:T(8,128)}, f32[108,64]{1,0:T(8,128)}, f32[32,32]{1,0:T(8,128)}, f32[32,32]{1,0:T(8,128)}, /*index=5*/f32[32,256]{1,0:T(8,128)}) custom-call(bf16[128,128]{1,0:T(8,128)(2,1)} %get-tuple-element.18.dense, f32[2048,128]{1,0:T(8,128)} %get-tuple-element.19.hot, ...), custom_call_target="tpu_custom_call" | custom-call | tf_op jit(solution)/shard_map/pallas_call | solution.py:662
  67.2 1.5 %copy.21 = f32[108,64]{0,1:T(8,128)} copy(f32[108,64]{1,0:T(8,128)} %get-tuple-element.38) | data formatting | bytes 55296

commit v3 on v2

--- a/solution.py
+++ b/solution.py
@@ -44,16 +44,16 @@
 
 
 def kernel(
-    act_hbm, hid_hbm, tw_hbm, x_hbm, bags, order, hot_in, dig_in, first_hbm, last_hbm, midq_ref,
+    act_hbm, hid_hbm, tw_hbm, x_hbm, bags, order, hot_in, dig_in, first_hbm, last_hbm, mid_hbm,
     dense_ref, hot_hbm, wout_ref, fout_ref, lout_ref, mout_ref,
-    act_ref, hid_ref, tw_ref, x_ref, first_ref, last_ref, midl, hot,
+    act_ref, hid_ref, tw_ref, x_ref, first_ref, last_ref, mid_block, mid_turned, midq, midl, hot,
     pooled, stage, meta, send_c, send_h, recv_c, recv_h, recv_m,
     xt, xt_recv, pre2, w_own, ring,
     first_t, last_t, onehot, a_t, c_t, q_t, he, ce, qs, tf, tl, mid_acc, mid_send, mid_recv,
-    fl_own, fl_send, fl_recv, fx, fx_recv,
-    wy, wy_recv, wz, wz_recv, fy, fy_recv, fz, fz_recv,
+    fl_own, fl_send, fl_recv, fa, fa_recv, fb, fb_recv, fa2, fa2_recv, fb2, fb2_recv,
+    wy, wy_recv, wz, wz_recv, fz, fz_recv,
     load_s, core_s, core_r, a_s, a_r, ring_s, ring_r, f_s, f_r, wy_s, wy_r, wz_s, wz_r,
-    fy_s, fy_r, fz_s, fz_r, m_s, m_r,
+    fz_s, fz_r, m_s, m_r,
 ):
     g = lax.axis_index("group")
     s = lax.axis_index("shard")
@@ -70,12 +70,14 @@
     load_tw = pltpu.make_async_copy(tw_hbm, tw_ref, load_s.at[3])
     load_first = pltpu.make_async_copy(first_hbm, first_ref, load_s.at[4])
     load_last = pltpu.make_async_copy(last_hbm, last_ref, load_s.at[5])
+    load_mid = pltpu.make_async_copy(mid_hbm.at[pl.ds(pl.multiple_of(s * 32, 32), 32)], mid_block, load_s.at[7])
     load_act.start()
     load_hid.start()
     load_x.start()
     load_tw.start()
     load_first.start()
     load_last.start()
+    load_mid.start()
 
     def shard_at(y, z, c):
         return y * 8 + z * 2 + c
@@ -110,33 +112,29 @@
     lax.fori_loop(1, GROUPS, greet_group, 0)
     lax.fori_loop(1, 4, greet_far, 0)
 
-    meta[...] = jnp.zeros_like(meta)
-    mine = lax.rem(s, 4)
-    hots = jnp.concatenate([hot_in[pl.ds(c, 8, stride=3), :] for c in range(3)], axis=1)
-
-    def place(values, width, i):
+    turns = lax.rem(s, 4)
+
+    def turned(values, width):
+        out = values
+        for n in range(1, 4):
+            out = jnp.where(turns == n, pltpu.roll(values, (4 - n) * width, 1), out)
+        return out
+
+    def kept(values, width, i):
+        low = lax.rem(i + 4 - turns, 4) * width
         lane = iota(values.shape, 1)
-        kept = jnp.where((lane >= i * width) & (lane < (i + 1) * width), values, 0)
-        out = kept
-        for j in range(4):
-            if j != i:
-                out = jnp.where(mine == j, pltpu.roll(kept, (j - i) % 4 * width, 1), out)
-        return out
-
+        return jnp.where((lane >= low) & (lane < low + width), values, 0)
+
+    hots = turned(jnp.concatenate([hot_in[pl.ds(c, 8, stride=3), :] for c in range(3)], axis=1), PER_HOT)
+    one_three = turned(dig_in[0:8, :] + dig_in[16:24, :] * 65536, PER_COLD)
+    two = turned(dig_in[8:16, :] % 32 * 65536, PER_COLD)
     for i in range(4):
-        out = place(hots, PER_HOT, i)
+        hot_i = kept(hots, PER_HOT, i)
+        rows = [hot_i[:, c * 128 : (c + 1) * 128] for c in range(3)] + [kept(one_three, PER_COLD, i)]
+        rows[0] = rows[0] + kept(two, PER_COLD, i)
         for q in range(8):
-            for c in range(3):
-                meta[4 * q + i, c : c + 1, :] = out[q : q + 1, c * 128 : (c + 1) * 128]
-    for r in range(3):
-        digit = dig_in[0, 0, r : r + 1, :]
-        if r == 1:
-            digit = digit % 32
-        digit = jnp.concatenate([digit[:, q * 128 : (q + 1) * 128] for q in range(8)], axis=0)
-        for i in range(4):
-            out = place(digit, PER_COLD, i)
-            for q in range(8):
-                meta[4 * q + i, 3 + r : 4 + r, :] = out[q : q + 1, :]
+            for c in range(4):
+                meta[4 * q + i, c : c + 1, :] = rows[c][q : q + 1, :]
 
     load_act.wait()
     load_hid.wait()
@@ -153,12 +151,6 @@
         pick = zero_one(iota((PAD_W, width), 1) == iota((PAD_W, width), 0) + off)
         xt[shard % 2, shard // 2] = dot_nt(pick, x_ref[:, lo : lo + width]).astype(BF16)
 
-    pl.semaphore_wait(barrier, SHARDS - 1 + GROUPS - 1 + 3)
-    send_pre = remote(pre2.at[0:128], pre2.at[128:256], core_s.at[0], core_r.at[0], partner)
-    send_pre.start()
-    send_xt = remote(xt.at[1 - core], xt_recv, core_s.at[1], core_r.at[1], partner)
-    send_xt.start()
-
     load_tw.wait()
     dense_ref[...] = dot_nt(pre, tw_ref[0:128, :]).astype(BF16)
     for i in range(13):
@@ -172,23 +164,38 @@
             stage[pl.ds(j, 1), :] = pooled[pl.ds(r, 1), :]
         return stage[0:count, :].astype(BF16)
 
+    def cold_for(k, carry):
+        o = lax.rem(s + k, SHARDS)
+        send_c[k] = gather(HOT_N + o * PER_COLD, PER_COLD)
+        return carry
+
+    lax.fori_loop(0, SHARDS, cold_for, 0)
+
+    pl.semaphore_wait(barrier, SHARDS - 1 + GROUPS - 1 + 3)
+    send_pre = remote(pre2.at[0:128], pre2.at[128:256], core_s.at[0], core_r.at[0], partner)
+    send_pre.start()
+    send_xt = remote(xt.at[1 - core], xt_recv, core_s.at[1], core_r.at[1], partner)
+    send_xt.start()
+
     def cold_to(k, carry):
         o = lax.rem(s + k, SHARDS)
-        send_c[k] = gather(HOT_N + o * PER_COLD, PER_COLD)
-        remote(send_c.at[k], recv_c.at[s], a_s.at[0], a_r.at[0], (g, o)).start()
-        remote(meta.at[o], recv_m.at[s], a_s.at[1], a_r.at[1], (g, o)).start()
-        return carry
+        remote(send_c.at[k], recv_c.at[k], a_s.at[0], a_r.at[0], (g, o)).start()
+        remote(meta.at[o], recv_m.at[k], a_s.at[1], a_r.at[1], (g, o)).start()
+        return carry
+
+    lax.fori_loop(1, SHARDS, cold_to, 0)
+    pltpu.make_async_copy(send_c.at[0], recv_c.at[0], a_r.at[0]).start()
+    pltpu.make_async_copy(meta.at[s], recv_m.at[0], a_r.at[1]).start()
 
     def hot_to(k, carry):
         o = lax.rem(s + k, SHARDS)
         send_h[k] = gather(o * PER_HOT, PER_HOT)
-        remote(send_h.at[k], recv_h.at[s], a_s.at[2], a_r.at[2], (g, o)).start()
-        return carry
-
-    lax.fori_loop(1, SHARDS, cold_to, 0)
-    send_c[0] = gather(HOT_N + s * PER_COLD, PER_COLD)
-    pltpu.make_async_copy(send_c.at[0], recv_c.at[s], a_r.at[0]).start()
-    pltpu.make_async_copy(meta.at[s], recv_m.at[s], a_r.at[1]).start()
+        remote(send_h.at[k], recv_h.at[k], a_s.at[2], a_r.at[2 + k // 8], (g, o)).start()
+        return carry
+
+    lax.fori_loop(1, SHARDS, hot_to, 0)
+    send_h[0] = gather(s * PER_HOT, PER_HOT)
+    pltpu.make_async_copy(send_h.at[0], recv_h.at[0], a_r.at[2]).start()
 
     send_pre.wait()
     send_xt.wait()
@@ -232,10 +239,6 @@
     for way in range(2):
         ring_copy(way, 0).start()
 
-    lax.fori_loop(1, SHARDS, hot_to, 0)
-    send_h[0] = gather(s * PER_HOT, PER_HOT)
-    pltpu.make_async_copy(send_h.at[0], recv_h.at[s], a_r.at[2]).start()
-
     load_first.wait()
     load_last.wait()
     eye = zero_one(iota((256, 256), 0) == iota((256, 256), 1))
@@ -243,22 +246,38 @@
     turn_row = iota((256, 256), 0)
     turn = zero_one(iota((256, 256), 1) == (turn_row % 32) * 8 + turn_row // 32)
     last_t[...] = dot_nt(turn, last_ref[...]).astype(BF16)
-    midl[...] = dot_nt(eye, midq_ref[...]).astype(BF16)
+    load_mid.wait()
+    block = mid_block[...].astype(F32)
+    sub = iota((8, 128), 0) % 4
+    apart = (sub + 4 - iota((8, 128), 1) // 32) % 4
+    for m0 in range(4):
+        for c in range(16):
+            value = block[m0 * 8 : (m0 + 1) * 8, c * 128 : (c + 1) * 128]
+            out = value
+            for d in range(1, 4):
+                moved = pltpu.roll(value, 128 - 32 * d, 1)
+                moved = jnp.where(sub >= d, pltpu.roll(moved, d, 0), pltpu.roll(moved, d + 4, 0))
+                out = jnp.where(apart == d, moved, out)
+            row = m0 * 64 + c * 4
+            mid_turned[row : row + 4, 0:128] = out[0:4]
+            mid_turned[row : row + 4, 128:256] = out[4:8]
+    source = turn_row // 64 * 64 + turn_row % 32 * 2 + turn_row // 32 % 2
+    midq[...] = dot(zero_one(iota((256, 256), 1) == source), mid_turned[...].astype(BF16)).astype(BF16)
+    midl[...] = dot_nt(eye, midq[...]).astype(BF16)
     mid_acc[...] = jnp.zeros_like(mid_acc)
-
-    ring_next(1)
 
     pltpu.make_async_copy(recv_c, recv_c, a_r.at[0]).wait()
     pltpu.make_async_copy(recv_m, recv_m, a_r.at[1]).wait()
 
-    def digits(t, row):
+    def words(t, row):
         four = recv_m[pl.ds(4 * t, 4), row : row + 1, :]
         return four[0] + four[1] + four[2] + four[3]
 
     def pick_cores(u, carry):
         lanes = pl.ds(pl.multiple_of(u * 256, 256), 256)
+        both = jnp.concatenate([words(2 * u, 3), words(2 * u + 1, 3)], axis=1)
         for i, (table, out) in enumerate(((first_t, a_t), (last_t, c_t))):
-            digit = jnp.concatenate([digits(2 * u, 3 + 2 * i), digits(2 * u + 1, 3 + 2 * i)], axis=1)
+            digit = both % 65536 if i == 0 else both // 65536
             for k in range(4):
                 row = iota((256, 256), 0) + k * 256
                 onehot[i, k * 256 : (k + 1) * 256, lanes] = zero_one(row == digit)
@@ -271,10 +290,10 @@
 
     def cold_tile(t, carry):
         lanes = pl.ds(pl.multiple_of(t * 128, 128), 128)
-        two = digits(t, 4)
+        two = words(t, 0) // 65536
         q_t[...] = recv_c[pl.ds(4 * t, 4)].reshape(128, 128).astype(F32).T
-        low = jnp.broadcast_to(jnp.concatenate([two % 4, two % 4], axis=1), (8, 256))
-        high = jnp.broadcast_to(jnp.concatenate([two // 4, two // 4], axis=1), (8, 256))
+        low = jnp.broadcast_to(jnp.concatenate([two // 8, two // 8], axis=1), (8, 256))
+        high = jnp.broadcast_to(jnp.concatenate([two % 8, two % 8], axis=1), (8, 256))
         is_low = [low == k for k in range(4)]
         is_high = [high == k for k in range(8)]
 
@@ -304,7 +323,7 @@
             c = c.astype(BF16).reshape(2, 16, 256)
             for k in range(8):
                 ce[k * 32 : (k + 1) * 32, cols] = (c * keep_high[k][None]).reshape(32, 256)
-            q_all = dot(midq_ref[...], ce[:, cols]).reshape(4, 8, 8, 256)
+            q_all = dot(midq[...], ce[:, cols]).reshape(4, 8, 8, 256)
             total = q_all[0]
             for k in range(1, 4):
                 total = jnp.where(is_low[k][None], q_all[k], total)
@@ -328,9 +347,10 @@
             tf[row : row + 32, lanes] = total.astype(BF16)
         return carry
 
-    lax.fori_loop(0, 4, cold_tile, 0)
+    ring_next(1)
+    lax.fori_loop(0, 5, cold_tile, 0)
     ring_next(2)
-    lax.fori_loop(4, 8, cold_tile, 0)
+    lax.fori_loop(5, 8, cold_tile, 0)
 
     row = iota((256, 256), 0)
     j = row % 32
@@ -397,22 +417,26 @@
         y_copy(wy, wy_recv, wy_s, wy_r, d).start()
 
     fl_copy.wait()
-
-    def fl_pair(j, carry):
-        for i in range(4):
-            fx[i, j] = (fl_own[core, i, j] + fl_recv[i, j].astype(F32)).astype(BF16)
-        return carry
-
-    lax.fori_loop(0, 16, fl_pair, 0)
-
-    def fl_x(d):
-        to = lax.rem(xx + d, 4)
-        return remote(fx.at[to], fx_recv.at[d - 1], f_s.at[d - 1], f_r.at[d - 1], (zh * 4 + to, s))
+    for y in range(4):
+        for z in range(4):
+            for k in range(4):
+                total = fl_own[core, k, 4 * y + z] + fl_recv[k, 4 * y + z].astype(F32)
+                if z < 2:
+                    fa[k, y, z] = total.astype(BF16)
+                else:
+                    fb[y, k, z - 2] = total.astype(BF16)
+
+    def f_copy(n, d):
+        by_x = n in (0, 3)
+        to = lax.rem((xx if by_x else yy) + d, 4)
+        device = (zh * 4 + to, s) if by_x else (g, shard_at(to, zl, core))
+        buf, into = ((fa, fa_recv), (fb, fb_recv), (fa2, fa2_recv), (fb2, fb2_recv))[n]
+        return remote(buf.at[to], into.at[d - 1], f_s.at[n, d - 1], f_r.at[n, d - 1], device)
 
     for d in range(1, 4):
-        fl_x(d).start()
-
-    pltpu.make_async_copy(recv_h, recv_h, a_r.at[2]).wait()
+        f_copy(0, d).start()
+        f_copy(1, d).start()
+
     hot[...] = jnp.zeros_like(hot)
 
     def hot_part(i, carry):
@@ -420,7 +444,7 @@
         for half in range(2):
             four = recv_m[pl.ds(8 * i + 4 * half, 4), :, :]
             four = four[0] + four[1] + four[2] + four[3]
-            ids += [four[k : k + 1, :] for k in range(3)]
+            ids += [four[k : k + 1, :] % 65536 for k in range(3)]
         values = recv_h[pl.ds(8 * i, 8)].reshape(768, 128).astype(F32)
         low = jnp.concatenate(ids, axis=1) % 512
         pick = zero_one(iota((512, 768), 0) == low)
@@ -434,23 +458,34 @@
             hot[(k + 1) * 512 : (k + 2) * 512, :] += part[:, 128:256]
         return carry
 
-    lax.fori_loop(0, 4, hot_part, 0)
-    save_hot = pltpu.make_async_copy(hot, hot_hbm, load_s.at[6])
-    save_hot.start()
+    def hot_group(i):
+        some = recv_h.at[8 * i : 8 * i + 8]
+        pltpu.make_async_copy(some, some, a_r.at[2 + i]).wait()
+        hot_part(i, 0)
+
+    hot_group(0)
+    hot_group(1)
 
     for d in range(1, 4):
-        fl_x(d).wait()
-
-    def fl_x_add(j, carry):
-        total = fx[xx, j].astype(F32)
-        for d in range(3):
-            total = total + fx_recv[d, j].astype(F32)
-        fy[j] = total.astype(BF16)
-        return carry
-
-    lax.fori_loop(0, 16, fl_x_add, 0)
+        f_copy(0, d).wait()
+    for n in range(4):
+        for z in range(2):
+            total = fa[xx, n, z].astype(F32)
+            for d in range(3):
+                total = total + fa_recv[d, n, z].astype(F32)
+            fa2[n, z] = total.astype(BF16)
     for d in range(1, 4):
-        y_copy(fy, fy_recv, fy_s, fy_r, d).start()
+        f_copy(2, d).start()
+    for d in range(1, 4):
+        f_copy(1, d).wait()
+    for n in range(4):
+        for z in range(2):
+            total = fb[yy, n, z].astype(F32)
+            for d in range(3):
+                total = total + fb_recv[d, n, z].astype(F32)
+            fb2[n, z] = total.astype(BF16)
+    for d in range(1, 4):
+        f_copy(3, d).start()
 
     for d in range(1, 4):
         y_copy(wy, wy_recv, wy_s, wy_r, d).wait()
@@ -476,16 +511,24 @@
     for d in range(1, 8):
         z_copy(wz, wz_recv, wz_s, wz_r, d).start()
 
+    hot_group(2)
+
     for d in range(1, 4):
-        y_copy(fy, fy_recv, fy_s, fy_r, d).wait()
+        f_copy(2, d).wait()
+        f_copy(3, d).wait()
     for j in range(4):
-        total = fy[4 * yy + j].astype(F32)
+        buf, into, at = (fa2, fa2_recv, yy) if j < 2 else (fb2, fb2_recv, xx)
+        total = buf[at, j % 2].astype(F32)
         for d in range(3):
-            total = total + fy_recv[d, j].astype(F32)
+            total = total + into[d, j % 2].astype(F32)
         for k, half in enumerate(halves(total, 16, 32)):
             fz[4 * k + j] = half.astype(BF16)
     for d in range(1, 8):
         z_copy(fz, fz_recv, fz_s, fz_r, d).start()
+
+    hot_group(3)
+    save_hot = pltpu.make_async_copy(hot, hot_hbm, load_s.at[6])
+    save_hot.start()
 
     for d in range(1, GROUPS):
         mid_copy(d).wait()
@@ -499,8 +542,9 @@
     total = wz[deep].astype(F32)
     for d in range(7):
         total = total + wz_recv[d].astype(F32)
-    wout_ref[0:56, :] = total[0:56, 0:64]
-    wout_ref[56:BLOCK_W, :] = pltpu.roll(total, 64, 1)[0 : BLOCK_W - 56, 0:64]
+    wout_ref[0:56, :] = total[0:56]
+    wout_ref[56:PAD_W, :] = pltpu.roll(total, 64, 1)[0:56]
+    wout_ref[PAD_W:128, :] = jnp.zeros((128 - PAD_W, 128), F32)
 
     for d in range(1, 8):
         z_copy(fz, fz_recv, fz_s, fz_r, d).wait()
@@ -524,7 +568,7 @@
 def finish(dense, hot, weight, first, last, mid, dense_out, hot_out, weight_out, first_out, last_out, mid_out):
     dense_out[...] = dense[...]
     hot_out[...] = hot[...]
-    weight_out[...] = weight[...]
+    weight_out[...] = weight[...].T[0:64, 0:BLOCK_W]
     first_out[...] = first[...]
     last_out[...] = last[...]
     for m1 in range(8):
@@ -533,7 +577,9 @@
             for e2 in range(2):
                 row = a * 8 + e2 * 4
                 parts.append(mid[row : row + 4, m1 * 32 : (m1 + 1) * 32])
-        mid_out[m1 * 4 : (m1 + 1) * 4, :] = jnp.concatenate(parts, axis=1)
+        rows = jnp.concatenate(parts, axis=1)
+        for m0 in range(4):
+            mid_out[m0 * 8 + m1 : m0 * 8 + m1 + 1, :] = rows[m0 : m0 + 1, :]
 
 
 def body(
@@ -549,10 +595,6 @@
     hot_rows,
     cold_digits,
 ):
-    s = lax.axis_index("shard")
-    block = lax.dynamic_slice_in_dim(core_mid, s * 32, 32, 0).reshape(8, 4, RANK, E2, RANK)
-    midq = block.transpose(1, 3, 2, 0, 4).reshape(256, 256)
-
     vmem = pl.BlockSpec(memory_space=pltpu.VMEM)
     smem = pl.BlockSpec(memory_space=pltpu.SMEM)
     hbm = pl.BlockSpec(memory_space=pl.ANY)
@@ -564,7 +606,7 @@
     shapes = (
         jax.ShapeDtypeStruct((128, 128), BF16),
         jax.ShapeDtypeStruct((2048, 128), F32),
-        jax.ShapeDtypeStruct((BLOCK_W, 64), F32),
+        jax.ShapeDtypeStruct((128, 128), F32),
         jax.ShapeDtypeStruct((32, 32), F32),
         jax.ShapeDtypeStruct((32, 32), F32),
         jax.ShapeDtypeStruct((32, 256), F32),
@@ -572,7 +614,7 @@
     outs = pl.pallas_call(
         kernel,
         out_shape=shapes,
-        in_specs=[hbm, hbm, hbm, hbm, smem, smem, vmem, vmem, hbm, hbm, vmem],
+        in_specs=[hbm, hbm, hbm, hbm, smem, smem, vmem, vmem, hbm, hbm, hbm],
         out_specs=(vmem, hbm, vmem, vmem, vmem, vmem),
         scratch_shapes=[
             buf(128, 512),
@@ -581,16 +623,19 @@
             buf(128, 3456),
             buf(1024, 256),
             buf(1024, 256),
+            buf(32, 2048),
+            buf(256, 256, dtype=F32),
+            buf(256, 256),
             buf(256, 256),
             buf(2048, 128, dtype=F32),
             buf(26 * 128, 128, dtype=F32),
             buf(PER_HOT, 128, dtype=F32),
-            buf(SHARDS, 8, 128, dtype=I32),
+            buf(SHARDS, 4, 128, dtype=I32),
             buf(SHARDS, PER_COLD, 128),
             buf(SHARDS, PER_HOT, 128),
             buf(SHARDS, PER_COLD, 128),
             buf(SHARDS, PER_HOT, 128),
-            buf(SHARDS, 8, 128, dtype=I32),
+            buf(SHARDS, 4, 128, dtype=I32),
             buf(2, 16, PAD_W, 128),
             buf(16, PAD_W, 128),
             buf(256, 512),
@@ -613,31 +658,33 @@
             buf(2, 4, 16, 32, 128, dtype=F32),
             buf(4, 16, 32, 128),
             buf(4, 16, 32, 128),
-            buf(4, 16, 32, 128),
-            buf(3, 16, 32, 128),
+            buf(4, 4, 2, 32, 128),
+            buf(3, 4, 2, 32, 128),
+            buf(4, 4, 2, 32, 128),
+            buf(3, 4, 2, 32, 128),
+            buf(4, 2, 32, 128),
+            buf(3, 2, 32, 128),
+            buf(4, 2, 32, 128),
+            buf(3, 2, 32, 128),
             buf(16, PAD_W, 128),
             buf(3, 4, PAD_W, 128),
             buf(8, 64, 128),
             buf(7, 64, 128),
-            buf(16, 32, 128),
-            buf(3, 4, 32, 128),
             buf(8, 16, 128),
             buf(7, 16, 128),
-            dma((7,)),
+            dma((8,)),
             dma((3,)),
             dma((3,)),
             dma((3,)),
-            dma((3,)),
+            dma((6,)),
             dma((2, 3)),
             dma((2, 3)),
-            dma((3,)),
-            dma((3,)),
+            dma((4, 3)),
+            dma((4, 3)),
             dma((3,)),
             dma((3,)),
             dma((7,)),
             dma((7,)),
-            dma((3,)),
-            dma((3,)),
             dma((7,)),
             dma((7,)),
             dma((7,)),
@@ -654,18 +701,18 @@
         bag_ids,
         lookup_order,
         hot_rows.reshape(24, 128),
-        cold_digits,
+        cold_digits.reshape(24, 128),
         core_first,
         core_last,
-        midq,
+        core_mid,
     )
     dense_grad, hot_grad, weight_grad, first_grad, last_grad, mid_grad = pl.pallas_call(
         finish,
-        out_shape=shapes,
+        out_shape=shapes[:2] + (jax.ShapeDtypeStruct((64, BLOCK_W), F32),) + shapes[3:],
         in_specs=[vmem] * 6,
         out_specs=(vmem,) * 6,
     )(*outs)
-    return (hot_grad[None], dense_grad, weight_grad, first_grad, mid_grad, last_grad)
+    return (hot_grad[None], dense_grad, weight_grad.T, first_grad, mid_grad, last_grad)
 
 
 def solution(mesh):

time: 69.2 us -> 66.7 us (0.964)
  local copies, waits for them, and re-layouts: 5.48 us -> 0 us
  Pallas kernels: 62.6 us -> 65.1 us
    unnamed x2 -> x0, local copies, waits for them, and re-layouts: 2.83 us -> none
    pallas_call x1, Pallas kernels: 60.2 us -> 62.7 us  [body(): pl.pallas_call(kernel, out_shape=shapes, in_specs=[hbm, hbm, hbm, hbm, sm...]
    reshape x2 -> x0, local copies, waits for them, and re-layouts: 1.39 us -> none  [the longest x1 1.02 us: body(): midq = block.transpose(1, 3, 2, 0, 4).reshape(256, 256)]
    dynamic_slice x1 -> x0, local copies, waits for them, and re-layouts: 0.91 us -> none  [body(): lax.dynamic_slice_in_dim(core_mid, s * 32, 32, 0)]
where the time goes in v3:
time: 66.7 us; the launch traced here: 65.7 us
  Pallas kernels  65.1 us (98%)
    pallas_call x1, Pallas kernels, body(): pl.pallas_call(kernel, out_shape=shapes, in_specs=[hbm, hbm, hbm, hbm, sm...  62.7 us
    pallas_call x1, Pallas kernels, body(): pl.pallas_call(finish, out_shape=shapes[:2] + (jax.ShapeDtypeStruct((64,...  2.34 us

profile of v3, /device:TPU:6, one launch (start us, length us, event | category | flops | bytes accessed | tf_op | source)
XLA Modules:
  0.0 65.7 jit_solution(14651409468317179656)
XLA Ops:
  0.6 62.7 %shard_map.154 = (bf16[128,128]{1,0:T(8,128)(2,1)}, f32[2048,128]{1,0:T(8,128)}, f32[128,128]{1,0:T(8,128)}, f32[32,32]{1,0:T(8,128)}, f32[32,32]{1,0:T(8,128)}, /*index=5*/f32[32,256]{1,0:T(8,128)}) custom-call(bf16[128,512]{1,0:T(8,128)(2,1)} %act_hbm.1, bf16[128,512]{1,0:T(8,128)(2,1)} %hid_hbm.1, bf16[3456,512]{1,0:T(8,128)(2,1)} %tw_hbm.1, ...), custom_call_target="tpu_custom_call" | custom-call | tf_op jit(solution)/shard_map/pallas_call | solution.py:614
  63.4 2.3 %shard_map.155 = (bf16[128,128]{1,0:T(8,128)(2,1)}, f32[2048,128]{1,0:T(8,128)}, f32[64,108]{1,0:T(8,128)}, f32[32,32]{1,0:T(8,128)}, f32[32,32]{1,0:T(8,128)}, /*index=5*/f32[32,256]{1,0:T(8,128)}) custom-call(bf16[128,128]{1,0:T(8,128)(2,1)} %get-tuple-element.18.dense, f32[2048,128]{1,0:T(8,128)} %get-tuple-element.19.hot, ...), custom_call_target="tpu_custom_call" | custom-call | tf_op jit(solution)/shard_map/pallas_call | solution.py:709

commit v4 on v3

--- a/solution.py
+++ b/solution.py
@@ -50,7 +50,7 @@
     pooled, stage, meta, send_c, send_h, recv_c, recv_h, recv_m,
     xt, xt_recv, pre2, w_own, ring,
     first_t, last_t, onehot, a_t, c_t, q_t, he, ce, qs, tf, tl, mid_acc, mid_send, mid_recv,
-    fl_own, fl_send, fl_recv, fa, fa_recv, fb, fb_recv, fa2, fa2_recv, fb2, fb2_recv,
+    fl_own, fl_send, fl_recv, fx, fx_sum, fx_recv,
     wy, wy_recv, wz, wz_recv, fz, fz_recv,
     load_s, core_s, core_r, a_s, a_r, ring_s, ring_r, f_s, f_r, wy_s, wy_r, wz_s, wz_r,
     fz_s, fz_r, m_s, m_r,
@@ -104,13 +104,14 @@
         return carry
 
     def greet_far(k, carry):
-        to = (lax.rem(g + 4, 8), shard_at(yy, lax.rem(zl + k, 4), core))
+        to = lax.rem(yy * 4 + zl + k, 16)
+        to = (lax.rem(g + 4, 8), shard_at(to // 4, lax.rem(to, 4), core))
         pl.semaphore_signal(barrier, inc=1, device_id=to, device_id_type=MESH)
         return carry
 
     lax.fori_loop(1, SHARDS, greet_shard, 0)
     lax.fori_loop(1, GROUPS, greet_group, 0)
-    lax.fori_loop(1, 4, greet_far, 0)
+    lax.fori_loop(1, 16, greet_far, 0)
 
     turns = lax.rem(s, 4)
 
@@ -171,7 +172,14 @@
 
     lax.fori_loop(0, SHARDS, cold_for, 0)
 
-    pl.semaphore_wait(barrier, SHARDS - 1 + GROUPS - 1 + 3)
+    def hot_for(k, carry):
+        o = lax.rem(s + k, SHARDS)
+        send_h[k] = gather(o * PER_HOT, PER_HOT)
+        return carry
+
+    lax.fori_loop(0, SHARDS, hot_for, 0)
+
+    pl.semaphore_wait(barrier, SHARDS - 1 + GROUPS - 1 + 15)
     send_pre = remote(pre2.at[0:128], pre2.at[128:256], core_s.at[0], core_r.at[0], partner)
     send_pre.start()
     send_xt = remote(xt.at[1 - core], xt_recv, core_s.at[1], core_r.at[1], partner)
@@ -186,16 +194,6 @@
     lax.fori_loop(1, SHARDS, cold_to, 0)
     pltpu.make_async_copy(send_c.at[0], recv_c.at[0], a_r.at[0]).start()
     pltpu.make_async_copy(meta.at[s], recv_m.at[0], a_r.at[1]).start()
-
-    def hot_to(k, carry):
-        o = lax.rem(s + k, SHARDS)
-        send_h[k] = gather(o * PER_HOT, PER_HOT)
-        remote(send_h.at[k], recv_h.at[k], a_s.at[2], a_r.at[2 + k // 8], (g, o)).start()
-        return carry
-
-    lax.fori_loop(1, SHARDS, hot_to, 0)
-    send_h[0] = gather(s * PER_HOT, PER_HOT)
-    pltpu.make_async_copy(send_h.at[0], recv_h.at[0], a_r.at[2]).start()
 
     send_pre.wait()
     send_xt.wait()
@@ -238,6 +236,14 @@
 
     for way in range(2):
         ring_copy(way, 0).start()
+
+    def hot_to(k, carry):
+        o = lax.rem(s + k, SHARDS)
+        remote(send_h.at[k], recv_h.at[k], a_s.at[2], a_r.at[2 + k // 8], (g, o)).start()
+        return carry
+
+    lax.fori_loop(1, 4, hot_to, 0)
+    pltpu.make_async_copy(send_h.at[0], recv_h.at[0], a_r.at[2]).start()
 
     load_first.wait()
     load_last.wait()
@@ -289,6 +295,7 @@
     lax.fori_loop(0, 4, pick_cores, 0)
 
     def cold_tile(t, carry):
+        lax.fori_loop(4 * t + 4, jnp.minimum(4 * t + 8, SHARDS), hot_to, 0)
         lanes = pl.ds(pl.multiple_of(t * 128, 128), 128)
         two = words(t, 0) // 65536
         q_t[...] = recv_c[pl.ds(4 * t, 4)].reshape(128, 128).astype(F32).T
@@ -348,9 +355,9 @@
         return carry
 
     ring_next(1)
-    lax.fori_loop(0, 5, cold_tile, 0)
+    lax.fori_loop(0, 6, cold_tile, 0)
     ring_next(2)
-    lax.fori_loop(5, 8, cold_tile, 0)
+    lax.fori_loop(6, 8, cold_tile, 0)
 
     row = iota((256, 256), 0)
     j = row % 32
@@ -370,18 +377,14 @@
             else:
                 part = jnp.where(lane < 64, pltpu.roll(a, 64, 1), b)
             for n in range(8):
-                fl_own[n % 2, i, 4 * k + n // 2] = part[n * 32 : (n + 1) * 32, :]
+                block = part[n * 32 : (n + 1) * 32, :]
+                fl_own[n % 2, i, 4 * k + n // 2] = block
+                fl_send[n % 2, i, 4 * k + n // 2] = block.astype(BF16)
         return carry
 
     lax.fori_loop(0, 4, by_digit, 0)
 
-    def fl_round(j, carry):
-        for i in range(4):
-            fl_send[i, j] = fl_own[1 - core, i, j].astype(BF16)
-        return carry
-
-    lax.fori_loop(0, 16, fl_round, 0)
-    fl_copy = remote(fl_send, fl_recv, core_s.at[2], core_r.at[2], partner)
+    fl_copy = remote(fl_send.at[1 - core], fl_recv, core_s.at[2], core_r.at[2], partner)
     fl_copy.start()
 
     row = iota((256, 256), 0)
@@ -417,25 +420,26 @@
         y_copy(wy, wy_recv, wy_s, wy_r, d).start()
 
     fl_copy.wait()
-    for y in range(4):
-        for z in range(4):
-            for k in range(4):
-                total = fl_own[core, k, 4 * y + z] + fl_recv[k, 4 * y + z].astype(F32)
-                if z < 2:
-                    fa[k, y, z] = total.astype(BF16)
-                else:
-                    fb[y, k, z - 2] = total.astype(BF16)
-
-    def f_copy(n, d):
-        by_x = n in (0, 3)
-        to = lax.rem((xx if by_x else yy) + d, 4)
-        device = (zh * 4 + to, s) if by_x else (g, shard_at(to, zl, core))
-        buf, into = ((fa, fa_recv), (fb, fb_recv), (fa2, fa2_recv), (fb2, fb2_recv))[n]
-        return remote(buf.at[to], into.at[d - 1], f_s.at[n, d - 1], f_r.at[n, d - 1], device)
-
-    for d in range(1, 4):
-        f_copy(0, d).start()
-        f_copy(1, d).start()
+
+    def fl_pair(j, carry):
+        for k in range(4):
+            fx[k, j] = (fl_own[core, k, j] + fl_recv[k, j].astype(F32)).astype(BF16)
+        return carry
+
+    lax.fori_loop(0, 16, fl_pair, 0)
+    next_x = (lax.rem(xx + 1, 4), lax.rem(xx + 3, 4))
+    far_x = lax.rem(xx + 2, 4)
+    low_half, high_half = pl.ds(0, 8), pl.ds(8, 8)
+
+    def f_copy(n):
+        way = n % 2
+        half = (low_half, high_half)[way]
+        rest = (high_half, low_half)[way]
+        src = (fx.at[far_x, half], fx.at[next_x[way], rest], fx_sum.at[way])[n // 2]
+        return remote(src, fx_recv.at[n], f_s.at[n], f_r.at[n], (right, left)[way])
+
+    for n in range(4):
+        f_copy(n).start()
 
     hot[...] = jnp.zeros_like(hot)
 
@@ -466,29 +470,18 @@
     hot_group(0)
     hot_group(1)
 
-    for d in range(1, 4):
-        f_copy(0, d).wait()
-    for n in range(4):
-        for z in range(2):
-            total = fa[xx, n, z].astype(F32)
-            for d in range(3):
-                total = total + fa_recv[d, n, z].astype(F32)
-            fa2[n, z] = total.astype(BF16)
-    for d in range(1, 4):
-        f_copy(2, d).start()
-    for d in range(1, 4):
-        f_copy(1, d).wait()
-    for n in range(4):
-        for z in range(2):
-            total = fb[yy, n, z].astype(F32)
-            for d in range(3):
-                total = total + fb_recv[d, n, z].astype(F32)
-            fb2[n, z] = total.astype(BF16)
-    for d in range(1, 4):
-        f_copy(3, d).start()
-
-    for d in range(1, 4):
-        y_copy(wy, wy_recv, wy_s, wy_r, d).wait()
+    for way in range(2):
+        f_copy(way).wait()
+
+        def way_add(j, carry):
+            total = fx[next_x[way], 8 * way + j].astype(F32) + fx_recv[way, j].astype(F32)
+            fx_sum[way, j] = total.astype(BF16)
+            return carry
+
+        lax.fori_loop(0, 8, way_add, 0)
+        f_copy(4 + way).start()
+
+    hot_group(2)
 
     def halves(total, count, width):
         top, bottom = total[0:count], total[count : 2 * count]
@@ -501,6 +494,29 @@
     def z_copy(buf, into, send_sem, recv_sem, d):
         to, device = along_z(d)
         return remote(buf.at[to], into.at[d - 1], send_sem.at[d - 1], recv_sem.at[d - 1], device)
+
+    for n in range(2, 6):
+        f_copy(n).wait()
+    for y in range(4):
+        for z in range(4):
+            at = 4 * y + z
+            way = at // 8
+            total = fx[xx, at].astype(F32) + fx_recv[3 - way, at % 8].astype(F32) + fx_recv[4 + way, at % 8].astype(F32)
+            for k, half in enumerate(halves(total, 16, 32)):
+                fz[8 * y + 4 * k + z] = half.astype(BF16)
+    here = yy * 8 + deep
+
+    def fz_to(d, carry):
+        to = lax.rem(here + d, 32)
+        z = lax.rem(to, 8)
+        device = ((z // 4) * 4 + xx, shard_at(to // 8, lax.rem(z, 4), core))
+        remote(fz.at[to], fz_recv.at[d], fz_s.at[0], fz_r.at[0], device).start()
+        return carry
+
+    lax.fori_loop(1, 32, fz_to, 0)
+
+    for d in range(1, 4):
+        y_copy(wy, wy_recv, wy_s, wy_r, d).wait()
 
     for j in range(4):
         total = wy[4 * yy + j].astype(F32)
@@ -511,21 +527,6 @@
     for d in range(1, 8):
         z_copy(wz, wz_recv, wz_s, wz_r, d).start()
 
-    hot_group(2)
-
-    for d in range(1, 4):
-        f_copy(2, d).wait()
-        f_copy(3, d).wait()
-    for j in range(4):
-        buf, into, at = (fa2, fa2_recv, yy) if j < 2 else (fb2, fb2_recv, xx)
-        total = buf[at, j % 2].astype(F32)
-        for d in range(3):
-            total = total + into[d, j % 2].astype(F32)
-        for k, half in enumerate(halves(total, 16, 32)):
-            fz[4 * k + j] = half.astype(BF16)
-    for d in range(1, 8):
-        z_copy(fz, fz_recv, fz_s, fz_r, d).start()
-
     hot_group(3)
     save_hot = pltpu.make_async_copy(hot, hot_hbm, load_s.at[6])
     save_hot.start()
@@ -546,16 +547,17 @@
     wout_ref[56:PAD_W, :] = pltpu.roll(total, 64, 1)[0:56]
     wout_ref[PAD_W:128, :] = jnp.zeros((128 - PAD_W, 128), F32)
 
-    for d in range(1, 8):
-        z_copy(fz, fz_recv, fz_s, fz_r, d).wait()
-    total = fz[deep].astype(F32)
-    for d in range(7):
+    arrived = fz_recv.at[1:32]
+    pltpu.make_async_copy(arrived, arrived, fz_r.at[0]).wait()
+    total = fz[here].astype(F32)
+    for d in range(1, 32):
         total = total + fz_recv[d].astype(F32)
     fout_ref[0:16, :] = total[:, 0:32]
     fout_ref[16:32, :] = pltpu.roll(total, 96, 1)[:, 0:32]
     lout_ref[0:16, :] = pltpu.roll(total, 64, 1)[:, 0:32]
     lout_ref[16:32, :] = pltpu.roll(total, 32, 1)[:, 0:32]
 
+    pltpu.make_async_copy(arrived, arrived, fz_s.at[0]).wait()
     save_hot.wait()
     sent = send_c.at[pl.ds(1, SHARDS - 1)]
     pltpu.make_async_copy(sent, sent, a_s.at[0]).wait()
@@ -656,22 +658,17 @@
             buf(8, 32, 256),
             buf(7, 32, 256),
             buf(2, 4, 16, 32, 128, dtype=F32),
+            buf(2, 4, 16, 32, 128),
             buf(4, 16, 32, 128),
             buf(4, 16, 32, 128),
-            buf(4, 4, 2, 32, 128),
-            buf(3, 4, 2, 32, 128),
-            buf(4, 4, 2, 32, 128),
-            buf(3, 4, 2, 32, 128),
-            buf(4, 2, 32, 128),
-            buf(3, 2, 32, 128),
-            buf(4, 2, 32, 128),
-            buf(3, 2, 32, 128),
+            buf(2, 8, 32, 128),
+            buf(6, 8, 32, 128),
             buf(16, PAD_W, 128),
             buf(3, 4, PAD_W, 128),
             buf(8, 64, 128),
             buf(7, 64, 128),
-            buf(8, 16, 128),
-            buf(7, 16, 128),
+            buf(32, 16, 128),
+            buf(32, 16, 128),
             dma((8,)),
             dma((3,)),
             dma((3,)),
@@ -679,14 +676,14 @@
             dma((6,)),
             dma((2, 3)),
             dma((2, 3)),
-            dma((4, 3)),
-            dma((4, 3)),
+            dma((6,)),
+            dma((6,)),
             dma((3,)),
             dma((3,)),
             dma((7,)),
             dma((7,)),
-            dma((7,)),
-            dma((7,)),
+            dma((1,)),
+            dma((1,)),
             dma((7,)),
             dma((7,)),
         ],

time: 66.7 us -> 63.4 us (0.951); the launches traced: 65.7 us -> 63.2 us
  Pallas kernels: 65.1 us -> 62.6 us
    pallas_call x1, Pallas kernels: 62.7 us -> 60.2 us  [body(): pl.pallas_call(kernel, out_shape=shapes, in_specs=[hbm, hbm, hbm, hbm, sm...]
where the time goes in v4:
time: 63.4 us; the launch traced here: 63.2 us
  Pallas kernels  62.6 us (99%)
  between operations  0.64 us (1%)
    pallas_call x1, Pallas kernels, body(): pl.pallas_call(kernel, out_shape=shapes, in_specs=[hbm, hbm, hbm, hbm, sm...  60.2 us
    pallas_call x1, Pallas kernels, body(): pl.pallas_call(finish, out_shape=shapes[:2] + (jax.ShapeDtypeStruct((64,...  2.34 us

profile of v4, /device:TPU:6, one launch (start us, length us, event | category | flops | bytes accessed | tf_op | source)
XLA Modules:
  0.0 63.2 jit_solution(12550176695043657265)
XLA Ops:
  0.6 60.2 %shard_map.154 = (bf16[128,128]{1,0:T(8,128)(2,1)}, f32[2048,128]{1,0:T(8,128)}, f32[128,128]{1,0:T(8,128)}, f32[32,32]{1,0:T(8,128)}, f32[32,32]{1,0:T(8,128)}, /*index=5*/f32[32,256]{1,0:T(8,128)}) custom-call(bf16[128,512]{1,0:T(8,128)(2,1)} %act_hbm.1, bf16[128,512]{1,0:T(8,128)(2,1)} %hid_hbm.1, bf16[3456,512]{1,0:T(8,128)(2,1)} %tw_hbm.1, ...), custom_call_target="tpu_custom_call" | custom-call | tf_op jit(solution)/shard_map/pallas_call | solution.py:616
  60.9 2.3 %shard_map.155 = (bf16[128,128]{1,0:T(8,128)(2,1)}, f32[2048,128]{1,0:T(8,128)}, f32[64,108]{1,0:T(8,128)}, f32[32,32]{1,0:T(8,128)}, f32[32,32]{1,0:T(8,128)}, /*index=5*/f32[32,256]{1,0:T(8,128)}) custom-call(bf16[128,128]{1,0:T(8,128)(2,1)} %get-tuple-element.18.dense, f32[2048,128]{1,0:T(8,128)} %get-tuple-element.19.hot, ...), custom_call_target="tpu_custom_call" | custom-call | tf_op jit(solution)/shard_map/pallas_call | solution.py:706

commit v5 on v4

--- a/solution.py
+++ b/solution.py
@@ -226,7 +226,7 @@
             ring[way, step, j] = total.astype(BF16)
             return carry
 
-        lax.fori_loop(0, 8, add, 0)
+        lax.fori_loop(0, 8, add, 0, unroll=4)
 
     def ring_next(step):
         for way in range(2):
@@ -292,7 +292,7 @@
             out[2 * u + 1] = part[:, 128:256]
         return carry
 
-    lax.fori_loop(0, 4, pick_cores, 0)
+    lax.fori_loop(0, 4, pick_cores, 0, unroll=2)
 
     def cold_tile(t, carry):
         lax.fori_loop(4 * t + 4, jnp.minimum(4 * t + 8, SHARDS), hot_to, 0)
@@ -382,7 +382,7 @@
                 fl_send[n % 2, i, 4 * k + n // 2] = block.astype(BF16)
         return carry
 
-    lax.fori_loop(0, 4, by_digit, 0)
+    lax.fori_loop(0, 4, by_digit, 0, unroll=2)
 
     fl_copy = remote(fl_send.at[1 - core], fl_recv, core_s.at[2], core_r.at[2], partner)
     fl_copy.start()
@@ -409,7 +409,7 @@
             wy[way * 8 + j] = total.astype(BF16)
             return carry
 
-        lax.fori_loop(0, 8, last_add, 0)
+        lax.fori_loop(0, 8, last_add, 0, unroll=4)
 
     def y_copy(buf, into, send_sem, recv_sem, d):
         to = lax.rem(yy + d, 4)
@@ -426,7 +426,7 @@
             fx[k, j] = (fl_own[core, k, j] + fl_recv[k, j].astype(F32)).astype(BF16)
         return carry
 
-    lax.fori_loop(0, 16, fl_pair, 0)
+    lax.fori_loop(0, 16, fl_pair, 0, unroll=4)
     next_x = (lax.rem(xx + 1, 4), lax.rem(xx + 3, 4))
     far_x = lax.rem(xx + 2, 4)
     low_half, high_half = pl.ds(0, 8), pl.ds(8, 8)
@@ -478,7 +478,7 @@
             fx_sum[way, j] = total.astype(BF16)
             return carry
 
-        lax.fori_loop(0, 8, way_add, 0)
+        lax.fori_loop(0, 8, way_add, 0, unroll=4)
         f_copy(4 + way).start()
 
     hot_group(2)

time: 63.4 us -> 63.4 us (level)
  no operation moved by 1% of the time
where the time goes in v5:
time: 63.4 us; the launch traced here: 63.1 us
  Pallas kernels  62.4 us (98%)
  between operations  0.64 us (1%)
    pallas_call x1, Pallas kernels, body(): pl.pallas_call(kernel, out_shape=shapes, in_specs=[hbm, hbm, hbm, hbm, sm...  60.1 us
    pallas_call x1, Pallas kernels, body(): pl.pallas_call(finish, out_shape=shapes[:2] + (jax.ShapeDtypeStruct((64,...  2.34 us

profile of v5, /device:TPU:6, one launch (start us, length us, event | category | flops | bytes accessed | tf_op | source)
XLA Modules:
  0.0 63.1 jit_solution(10366965556882361449)
XLA Ops:
  0.6 60.1 %shard_map.154 = (bf16[128,128]{1,0:T(8,128)(2,1)}, f32[2048,128]{1,0:T(8,128)}, f32[128,128]{1,0:T(8,128)}, f32[32,32]{1,0:T(8,128)}, f32[32,32]{1,0:T(8,128)}, /*index=5*/f32[32,256]{1,0:T(8,128)}) custom-call(bf16[128,512]{1,0:T(8,128)(2,1)} %act_hbm.1, bf16[128,512]{1,0:T(8,128)(2,1)} %hid_hbm.1, bf16[3456,512]{1,0:T(8,128)(2,1)} %tw_hbm.1, ...), custom_call_target="tpu_custom_call" | custom-call | tf_op jit(solution)/shard_map/pallas_call | solution.py:616
  60.7 2.3 %shard_map.155 = (bf16[128,128]{1,0:T(8,128)(2,1)}, f32[2048,128]{1,0:T(8,128)}, f32[64,108]{1,0:T(8,128)}, f32[32,32]{1,0:T(8,128)}, f32[32,32]{1,0:T(8,128)}, /*index=5*/f32[32,256]{1,0:T(8,128)}) custom-call(bf16[128,128]{1,0:T(8,128)(2,1)} %get-tuple-element.18.dense, f32[2048,128]{1,0:T(8,128)} %get-tuple-element.19.hot, ...), custom_call_target="tpu_custom_call" | custom-call | tf_op jit(solution)/shard_map/pallas_call | solution.py:706
